TPU v7x, 32 devices: a whole 2x2x4 slice. The times are simulated.
32 devices in a mesh: blk: 16 (over z, x, core), slab: 2 (over y).
Axes of the slice: x: 2, y: 2, z: 4, core: 2. Of those that a mesh axis runs over, the one named last changes fastest.
Arguments:
- tokens: bfloat16 [524288, 128], P(('blk', 'slab')), may hold values from -6 to 6
- listed: int32 [2048, 3], P(('blk', 'slab')), may hold values from 0 to 511, as said below
- centroids: bfloat16 [131072, 128], P('blk'), may hold values from -6 to 6
Outputs:
- refined: float32 [131072, 128], P(('blk', 'slab'))
- counts: float32 [131072], P(('blk', 'slab'))
Inputs may be any that keep to these rules, and one draw needn't show every extreme that they name: `listed`: in the rows of one device (64 token blocks), all ids of one owner group (id // 32) are equal, so a device names at most one block of each owner group. The three ids of a row are distinct.
All inputs are finite; a program needn't handle non-finite values.
Results may differ from a plain program's by a relative error of at most 0.00093.
Values may be sent and summed in bfloat16 or wider, within the bound.
A program may use at most 128 MiB of HBM per device.

v0:
```python
import jax
import jax.numpy as jnp
from jax import lax
from jax.sharding import PartitionSpec as P

EMBED_WIDTH = 128
CENT_BLK = 256
TOK_BLK = 256
BPO = 32


SOFTMAX_TEMP = 0.1
PRIOR_WEIGHT = 4.0
EPSILON = 1e-06


def unit_rows(values):
    widened = values.astype(jnp.float32)
    return widened * lax.rsqrt(jnp.mean(widened * widened, axis=-1, keepdims=True) + EPSILON)


def finish_sums(back_sums, back_counts, asked_ids):
    pick_rows = (asked_ids[:, None] == jnp.arange(BPO, dtype=jnp.int32)).astype(jnp.float32)
    own_sums = jnp.einsum("js,jcd->scd", pick_rows, back_sums, precision=lax.Precision.HIGHEST)
    own_counts = jnp.einsum("js,jc->sc", pick_rows, back_counts, precision=lax.Precision.HIGHEST)
    mine_sums, mine_counts = (
        lax.psum_scatter(own_sums, "slab", scatter_dimension=0, tiled=True),
        lax.psum_scatter(own_counts, "slab", scatter_dimension=0, tiled=True),
    )
    return (mine_sums, mine_counts)


def shards(tokens, listed, centroids):
    owner_count = lax.axis_size("blk")
    slab_number_count = lax.axis_size("slab")
    slab_index = lax.axis_index("slab")
    centroid_norm = unit_rows(centroids).reshape(BPO, CENT_BLK, EMBED_WIDTH)
    cent_send = centroid_norm.astype(jnp.bfloat16)
    tok_norm = unit_rows(tokens).astype(jnp.bfloat16).reshape(-1, TOK_BLK, EMBED_WIDTH)
    block_count = tok_norm.shape[0]
    owner_ids = jnp.arange(owner_count, dtype=jnp.int32)
    group_of = listed // BPO
    inner_ids = listed % BPO
    matches = group_of[:, :, None] == owner_ids
    wanted = jnp.max(jnp.where(matches, inner_ids[:, :, None] + 1, 0), axis=(0, 1)) - 1
    request_rows = lax.all_gather(wanted.reshape(1, owner_count), "blk", axis=0, tiled=True)
    asked_ids = lax.dynamic_index_in_dim(request_rows, lax.axis_index("blk"), 1, keepdims=False)
    replies = cent_send[jnp.maximum(asked_ids, 0)]
    fetched = lax.all_to_all(replies, "blk", split_axis=0, concat_axis=0, tiled=True)
    group_size = min(16, block_count)
    turn_count = block_count // group_size

    def accumulate(state_pair, turn_index):
        sum_acc, count_acc = state_pair
        start = turn_index * group_size
        token_rows = lax.dynamic_slice_in_dim(tok_norm, start, group_size, 0)
        slot_ids = lax.dynamic_slice_in_dim(group_of, start, group_size, 0)
        candidate_centroids = fetched[slot_ids].reshape(group_size, 3 * CENT_BLK, EMBED_WIDTH)
        score_matrix = jnp.einsum(
            "wsy,way->wsa", token_rows, candidate_centroids, preferred_element_type=jnp.float32
        ) / (EMBED_WIDTH * SOFTMAX_TEMP)
        weights = jnp.exp(score_matrix)
        weights = weights / jnp.sum(weights, axis=-1, keepdims=True)
        weights_low = weights.astype(jnp.bfloat16).reshape(group_size, TOK_BLK, 3, CENT_BLK)
        partial_value = jnp.einsum(
            "gtkc,gtd->gkcd", weights_low, token_rows, preferred_element_type=jnp.float32
        )
        part_counts = jnp.sum(weights.reshape(group_size, TOK_BLK, 3, CENT_BLK), axis=1)
        one_hot = (slot_ids.reshape(-1)[:, None] == owner_ids).astype(jnp.float32)
        sum_acc = sum_acc + jnp.einsum(
            "ns,ncd->scd",
            one_hot,
            partial_value.reshape(-1, CENT_BLK, EMBED_WIDTH),
            precision=lax.Precision.HIGHEST,
        )
        count_acc = count_acc + jnp.einsum(
            "ns,nc->sc", one_hot, part_counts.reshape(-1, CENT_BLK), precision=lax.Precision.HIGHEST
        )
        return ((sum_acc, count_acc), None)

    start_pair = (
        jnp.zeros((owner_count, CENT_BLK, EMBED_WIDTH), jnp.float32),
        jnp.zeros((owner_count, CENT_BLK), jnp.float32),
    )
    (sum_acc, count_acc), _ = lax.scan(
        accumulate, start_pair, jnp.arange(turn_count, dtype=jnp.int32)
    )
    back_sums, back_counts = (
        lax.all_to_all(sum_acc, "blk", split_axis=0, concat_axis=0, tiled=True),
        lax.all_to_all(count_acc, "blk", split_axis=0, concat_axis=0, tiled=True),
    )
    mine_sums, mine_counts = finish_sums(back_sums, back_counts, asked_ids)
    share_blocks = BPO // slab_number_count
    mine_cent = lax.dynamic_slice_in_dim(centroid_norm, slab_index * share_blocks, share_blocks, 0)
    refined = (mine_sums + PRIOR_WEIGHT * mine_cent) / (mine_counts[:, :, None] + PRIOR_WEIGHT)
    return (
        refined.reshape(share_blocks * CENT_BLK, EMBED_WIDTH),
        mine_counts.reshape(share_blocks * CENT_BLK),
    )


def solution(mesh):
    placed = (P(("blk", "slab"), None), P(("blk", "slab"), None), P("blk", None))
    return jax.shard_map(
        shards,
        mesh=mesh,
        in_specs=placed,
        out_specs=(P(("blk", "slab"), None), P(("blk", "slab"))),
        check_vma=False,
    )
```

profile of v0, /device:TPU:0, one launch (start us, length us, event | category | flops | bytes accessed | tf_op | source)
XLA Modules:
  0.0 334.2 jit_solution(10260862147334782899)
XLA Ops:
  7.2 0.7 fusion.35
  7.9 1.2 dynamic-slice
  10.1 13.9 %all-reduce.1 = s32[16,16]{1,0:T(8,128)S(1)} all-reduce(s32[16,16]{1,0:T(8,128)S(1)} %reshape.90), channel_id=2, replica_groups=mesh['blk'=16,'slab'=2] {'blk'}, use_global_device_ids=true, to_apply=%add | all-reduce | flops 256 | bytes 2048
  24.0 0.2 dynamic-slice_reduce_fusion
  24.2 2.7 fusion.23
  26.9 4.6 %convert_multiply_fusion.2 = f32[8192,128]{1,0:T(8,128)S(1)} fusion(bf16[8192,128]{1,0:T(8,128)(2,1)} %param.7, f32[8192]{0:T(1024)S(1)} %add_rsqrt_fusion.1), kind=kLoop, calls=%fused_computation.30 | loop fusion | flops 2097152 | bytes 6324224 | tf_op jit(solution)/shard_map/mul | solution.py:19
  31.5 1.9 copy-done.4
  33.5 0.3 convert_element_type.20
  33.8 1.7 gather_fusion.1
  35.5 3.7 %all-to-all-start = ((bf16[16,256,128]{2,1,0:T(8,128)(2,1)}), bf16[16,256,128]{2,1,0:T(8,128)(2,1)S(1)}, u32[]{:S(2)}, u32[]{:S(2)}) async-start(bf16[16,256,128]{2,1,0:T(8,128)(2,1)} %gather_fusion.1), calls=%async_computation | async-start | bytes 2097152 | tf_op jit(solution)/shard_map/all_to_all | solution.py:49
  39.1 4.1 %fusion.21 = f32[16384]{0:T(1024)S(1)} fusion(bf16[16384,128]{1,0:T(8,128)(2,1)} %param.5), kind=kLoop, calls=%fused_computation.28 | loop fusion | flops 6275072 | bytes 4259840 | tf_op jit(solution)/shard_map/reduce_sum | solution.py:19
  43.3 7.8 %fusion.22 = bf16[16384,128]{1,0:T(8,128)(2,1)} fusion(bf16[16384,128]{1,0:T(8,128)(2,1)S(1)} %copy-done.5, f32[16384]{0:T(1024)S(1)} %add_rsqrt_fusion), kind=kLoop, calls=%fused_computation.29 | loop fusion | flops 6291456 | bytes 8454144 | tf_op jit(solution)/shard_map/convert_element_type | solution.py:39
  51.1 10.9 %all-to-all-done = bf16[16,256,128]{2,1,0:T(8,128)(2,1)S(1)} async-done(((bf16[16,256,128]{2,1,0:T(8,128)(2,1)}), bf16[16,256,128]{2,1,0:T(8,128)(2,1)S(1)}, u32[]{:S(2)}, u32[]{:S(2)}) %all-to-all-start) | async-done | bytes 1048608 | tf_op jit(solution)/shard_map/all_to_all | solution.py:49
  62.0 134.8 %while.13 = (s32[]{:T(128)}, f32[16,256,128]{2,0,1:T(8,128)}, f32[16,256]{1,0:T(8,128)S(1)}, s32[4]{0:T(128)S(1)}, s32[64,3]{0,1:T(4,128)S(1)}, /*index=5*/bf16[...) while((s32[]{:T(128)}, f32[16,256,128]{2,0,1:T(8,128)}, ...), condition=%wide.region_6.7_spmd.clone, body=%wide.region_3.6_spmd.clone.sunk | while | flops 1934879360 | bytes 104078264 | solution.py:85
  62.0 0.7 dynamic_slice.41
  63.8 2.4 gather_fusion
  66.2 3.4 %fusion.55 = (f32[16,256]{1,0:T(8,128)S(1)}, f32[16,256,768]{2,1,0:T(8,128)S(1)}) fusion(bf16[16,768,128]{2,1,0:T(8,128)(2,1)S(1)} %bitcast.47, bf16[64,256,128]{2,1,0:T(8,128)(2,1)} %get-tuple-element.187, s32[]{:T(128)S(6)} %select_n.47), kind=kOutput, calls=%fused_computation.5.clone.1 | convolution fusion | flops 811593728 | bytes 16793604 | tf_op jit(solution)/shard_map/while/body/eval_jaxpr/wsy,way->wsa/dot_general | solution.py:59
  69.6 4.9 %fusion.56 = (f32[16,768]{1,0:T(8,128)S(1)}, bf16[16,256,768]{2,1,0:T(8,128)(2,1)}) fusion(f32[16,256]{1,0:T(8,128)S(1)} %get-tuple-element.156, f32[16,256,768]{2,1,0:T(8,128)S(1)} %get-tuple-element.157), kind=kLoop, calls=%fused_computation.8.clone.1 | loop fusion | flops 12570624 | bytes 18939904 | tf_op jit(solution)/shard_map/while/body/eval_jaxpr/reduce_sum | solution.py:68
  74.5 8.6 %copy.88 = bf16[16,256,768]{1,2,0:T(8,128)(2,1)} copy(bf16[16,256,768]{2,1,0:T(8,128)(2,1)} %get-tuple-element.158) | data formatting | bytes 12582912 | tf_op jit(solution)/shard_map/while/body/eval_jaxpr/convert_element_type | solution.py:64
  83.1 5.0 %fusion.57 = f32[16,3,256,128]{3,2,1,0:T(8,128)S(1)} fusion(bf16[16,256,3,256]{1,3,2,0:T(8,128)(2,1)} %bitcast.45, bf16[64,256,128]{2,1,0:T(8,128)(2,1)} %get-tuple-element.187, s32[]{:T(128)S(6)} %select_n.47), kind=kOutput, calls=%fused_computation.12.clone.1 | convolution fusion | flops 805306368 | bytes 13631492 | tf_op jit(solution)/shard_map/while/body/eval_jaxpr/gtkc,gtd->gkcd/dot_general | solution.py:65
  88.1 6.2 %select_add_fusion.2 = f32[16,256,128]{2,0,1:T(8,128)S(1)} fusion(f32[16,256,128]{2,0,1:T(8,128)S(1)} %copy-done.2, f32[48,256,128]{2,1,0:T(8,128)S(1)} %bitcast.46, pred[]{:T(512)S(6)} %compare.6, s32[48]{0:T(128)S(1)} %eq.103), kind=kOutput, calls=%fused_computation.10.clone.1 | convolution fusion | flops 303039232 | bytes 10485953 | tf_op jit(solution)/shard_map/while/body/eval_jaxpr/ns,ncd->scd/dot_general | solution.py:70
  94.4 0.1 convolution_add_fusion.2
  94.6 1.2 copy-done.3
  95.7 0.7 dynamic_slice.41
  97.5 2.4 gather_fusion
  99.9 3.4 %fusion.55 = (f32[16,256]{1,0:T(8,128)S(1)}, f32[16,256,768]{2,1,0:T(8,128)S(1)}) fusion(bf16[16,768,128]{2,1,0:T(8,128)(2,1)S(1)} %bitcast.47, bf16[64,256,128]{2,1,0:T(8,128)(2,1)} %get-tuple-element.187, s32[]{:T(128)S(6)} %select_n.47), kind=kOutput, calls=%fused_computation.5.clone.1 | convolution fusion | flops 811593728 | bytes 16793604 | tf_op jit(solution)/shard_map/while/body/eval_jaxpr/wsy,way->wsa/dot_general | solution.py:59
  103.3 4.9 %fusion.56 = (f32[16,768]{1,0:T(8,128)S(1)}, bf16[16,256,768]{2,1,0:T(8,128)(2,1)}) fusion(f32[16,256]{1,0:T(8,128)S(1)} %get-tuple-element.156, f32[16,256,768]{2,1,0:T(8,128)S(1)} %get-tuple-element.157), kind=kLoop, calls=%fused_computation.8.clone.1 | loop fusion | flops 12570624 | bytes 18939904 | tf_op jit(solution)/shard_map/while/body/eval_jaxpr/reduce_sum | solution.py:68
  108.2 8.6 %copy.88 = bf16[16,256,768]{1,2,0:T(8,128)(2,1)} copy(bf16[16,256,768]{2,1,0:T(8,128)(2,1)} %get-tuple-element.158) | data formatting | bytes 12582912 | tf_op jit(solution)/shard_map/while/body/eval_jaxpr/convert_element_type | solution.py:64
  116.8 5.0 %fusion.57 = f32[16,3,256,128]{3,2,1,0:T(8,128)S(1)} fusion(bf16[16,256,3,256]{1,3,2,0:T(8,128)(2,1)} %bitcast.45, bf16[64,256,128]{2,1,0:T(8,128)(2,1)} %get-tuple-element.187, s32[]{:T(128)S(6)} %select_n.47), kind=kOutput, calls=%fused_computation.12.clone.1 | convolution fusion | flops 805306368 | bytes 13631492 | tf_op jit(solution)/shard_map/while/body/eval_jaxpr/gtkc,gtd->gkcd/dot_general | solution.py:65
  121.8 6.2 %select_add_fusion.2 = f32[16,256,128]{2,0,1:T(8,128)S(1)} fusion(f32[16,256,128]{2,0,1:T(8,128)S(1)} %copy-done.2, f32[48,256,128]{2,1,0:T(8,128)S(1)} %bitcast.46, pred[]{:T(512)S(6)} %compare.6, s32[48]{0:T(128)S(1)} %eq.103), kind=kOutput, calls=%fused_computation.10.clone.1 | convolution fusion | flops 303039232 | bytes 10485953 | tf_op jit(solution)/shard_map/while/body/eval_jaxpr/ns,ncd->scd/dot_general | solution.py:70
  128.1 0.1 convolution_add_fusion.2
  128.3 1.2 copy-done.3
  129.4 0.7 dynamic_slice.41
  131.2 2.4 gather_fusion
  133.6 3.4 %fusion.55 = (f32[16,256]{1,0:T(8,128)S(1)}, f32[16,256,768]{2,1,0:T(8,128)S(1)}) fusion(bf16[16,768,128]{2,1,0:T(8,128)(2,1)S(1)} %bitcast.47, bf16[64,256,128]{2,1,0:T(8,128)(2,1)} %get-tuple-element.187, s32[]{:T(128)S(6)} %select_n.47), kind=kOutput, calls=%fused_computation.5.clone.1 | convolution fusion | flops 811593728 | bytes 16793604 | tf_op jit(solution)/shard_map/while/body/eval_jaxpr/wsy,way->wsa/dot_general | solution.py:59
  137.0 4.9 %fusion.56 = (f32[16,768]{1,0:T(8,128)S(1)}, bf16[16,256,768]{2,1,0:T(8,128)(2,1)}) fusion(f32[16,256]{1,0:T(8,128)S(1)} %get-tuple-element.156, f32[16,256,768]{2,1,0:T(8,128)S(1)} %get-tuple-element.157), kind=kLoop, calls=%fused_computation.8.clone.1 | loop fusion | flops 12570624 | bytes 18939904 | tf_op jit(solution)/shard_map/while/body/eval_jaxpr/reduce_sum | solution.py:68
  141.9 8.6 %copy.88 = bf16[16,256,768]{1,2,0:T(8,128)(2,1)} copy(bf16[16,256,768]{2,1,0:T(8,128)(2,1)} %get-tuple-element.158) | data formatting | bytes 12582912 | tf_op jit(solution)/shard_map/while/body/eval_jaxpr/convert_element_type | solution.py:64
  150.5 5.0 %fusion.57 = f32[16,3,256,128]{3,2,1,0:T(8,128)S(1)} fusion(bf16[16,256,3,256]{1,3,2,0:T(8,128)(2,1)} %bitcast.45, bf16[64,256,128]{2,1,0:T(8,128)(2,1)} %get-tuple-element.187, s32[]{:T(128)S(6)} %select_n.47), kind=kOutput, calls=%fused_computation.12.clone.1 | convolution fusion | flops 805306368 | bytes 13631492 | tf_op jit(solution)/shard_map/while/body/eval_jaxpr/gtkc,gtd->gkcd/dot_general | solution.py:65
  155.5 6.2 %select_add_fusion.2 = f32[16,256,128]{2,0,1:T(8,128)S(1)} fusion(f32[16,256,128]{2,0,1:T(8,128)S(1)} %copy-done.2, f32[48,256,128]{2,1,0:T(8,128)S(1)} %bitcast.46, pred[]{:T(512)S(6)} %compare.6, s32[48]{0:T(128)S(1)} %eq.103), kind=kOutput, calls=%fused_computation.10.clone.1 | convolution fusion | flops 303039232 | bytes 10485953 | tf_op jit(solution)/shard_map/while/body/eval_jaxpr/ns,ncd->scd/dot_general | solution.py:70
  161.8 0.1 convolution_add_fusion.2
  162.0 1.2 copy-done.3
  163.1 0.7 dynamic_slice.41
  164.9 2.4 gather_fusion
  167.3 3.4 %fusion.55 = (f32[16,256]{1,0:T(8,128)S(1)}, f32[16,256,768]{2,1,0:T(8,128)S(1)}) fusion(bf16[16,768,128]{2,1,0:T(8,128)(2,1)S(1)} %bitcast.47, bf16[64,256,128]{2,1,0:T(8,128)(2,1)} %get-tuple-element.187, s32[]{:T(128)S(6)} %select_n.47), kind=kOutput, calls=%fused_computation.5.clone.1 | convolution fusion | flops 811593728 | bytes 16793604 | tf_op jit(solution)/shard_map/while/body/eval_jaxpr/wsy,way->wsa/dot_general | solution.py:59
  170.7 4.9 %fusion.56 = (f32[16,768]{1,0:T(8,128)S(1)}, bf16[16,256,768]{2,1,0:T(8,128)(2,1)}) fusion(f32[16,256]{1,0:T(8,128)S(1)} %get-tuple-element.156, f32[16,256,768]{2,1,0:T(8,128)S(1)} %get-tuple-element.157), kind=kLoop, calls=%fused_computation.8.clone.1 | loop fusion | flops 12570624 | bytes 18939904 | tf_op jit(solution)/shard_map/while/body/eval_jaxpr/reduce_sum | solution.py:68
  175.6 8.6 %copy.88 = bf16[16,256,768]{1,2,0:T(8,128)(2,1)} copy(bf16[16,256,768]{2,1,0:T(8,128)(2,1)} %get-tuple-element.158) | data formatting | bytes 12582912 | tf_op jit(solution)/shard_map/while/body/eval_jaxpr/convert_element_type | solution.py:64
  184.2 5.0 %fusion.57 = f32[16,3,256,128]{3,2,1,0:T(8,128)S(1)} fusion(bf16[16,256,3,256]{1,3,2,0:T(8,128)(2,1)} %bitcast.45, bf16[64,256,128]{2,1,0:T(8,128)(2,1)} %get-tuple-element.187, s32[]{:T(128)S(6)} %select_n.47), kind=kOutput, calls=%fused_computation.12.clone.1 | convolution fusion | flops 805306368 | bytes 13631492 | tf_op jit(solution)/shard_map/while/body/eval_jaxpr/gtkc,gtd->gkcd/dot_general | solution.py:65
  189.2 6.2 %select_add_fusion.2 = f32[16,256,128]{2,0,1:T(8,128)S(1)} fusion(f32[16,256,128]{2,0,1:T(8,128)S(1)} %copy-done.2, f32[48,256,128]{2,1,0:T(8,128)S(1)} %bitcast.46, pred[]{:T(512)S(6)} %compare.6, s32[48]{0:T(128)S(1)} %eq.103), kind=kOutput, calls=%fused_computation.10.clone.1 | convolution fusion | flops 303039232 | bytes 10485953 | tf_op jit(solution)/shard_map/while/body/eval_jaxpr/ns,ncd->scd/dot_general | solution.py:70
  195.5 0.1 convolution_add_fusion.2
  195.7 1.2 copy-done.3
  196.8 0.6 all_to_all.16
  197.4 6.8 %all-to-all-start.2 = ((f32[16,1,256]{2,1,0:T(1,128)}), f32[16,1,256]{2,1,0:T(1,128)S(1)}, u32[]{:S(2)}, u32[]{:S(2)}) async-start(f32[16,1,256]{2,1,0:T(1,128)} %all_to_all.16), calls=%async_computation.3 | async-start | bytes 32768 | tf_op jit(solution)/shard_map/all_to_all | solution.py:90
  204.3 3.6 %copy.58 = f32[16,256,128]{2,1,0:T(8,128)} copy(f32[16,256,128]{2,0,1:T(8,128)} %get-tuple-element.45) | data formatting | bytes 4194304 | tf_op jit(solution)/shard_map/while | solution.py:85
  207.9 2.9 all-to-all-done.2
  210.8 3.7 %all-to-all-start.1 = ((f32[16,256,128]{2,1,0:T(8,128)}), f32[16,256,128]{2,1,0:T(8,128)S(1)}, u32[]{:S(2)}, u32[]{:S(2)}) async-start(f32[16,256,128]{2,1,0:T(8,128)} %copy.58), calls=%async_computation.1 | async-start | bytes 4194304 | tf_op jit(solution)/shard_map/all_to_all | solution.py:89
  214.5 0.9 fusion.28
  215.5 40.0 %all-to-all-done.1 = f32[16,256,128]{2,1,0:T(8,128)S(1)} async-done(((f32[16,256,128]{2,1,0:T(8,128)}), f32[16,256,128]{2,1,0:T(8,128)S(1)}, u32[]{:S(2)}, u32[]{:S(2)}) %all-to-all-start.1) | async-done | bytes 2097184 | tf_op jit(solution)/shard_map/all_to_all | solution.py:89
  255.5 5.0 %fusion.26 = f32[32,256,128]{2,0,1:T(8,128)} fusion(f32[16,256,128]{2,1,0:T(8,128)S(1)} %all-to-all-done.1, s32[16]{0:T(128)S(1)} %get-tuple-element.87), kind=kOutput, calls=%fused_computation.36 | convolution fusion | flops 201327104 | bytes 6291520 | tf_op jit(solution)/shard_map/js,jcd->scd/dot_general | solution.py:24
  260.5 1.7 constant_dynamic-slice_fusion.1
  262.3 1.3 copy.67
  263.6 0.7 broadcast_add_fusion
  264.4 57.1 %reduce-scatter.3.cloned.1.call-done = f32[16,256,128]{2,0,1:T(8,128)} async-done(((f32[32,256,128]{2,0,1:T(8,128)}), f32[16,256,128]{2,0,1:T(8,128)}) %reduce-scatter.3.cloned.1.call-update) | async-done | bytes 2097168 | tf_op jit(solution)/shard_map/reduce_scatter | solution.py:27
  321.5 3.9 %fusion.25 = f32[16,256,128]{2,0,1:T(8,128)S(1)} fusion(f32[16,256,128]{2,0,1:T(8,128)} %reduce-scatter.3.cloned.1.call-done, f32[16,256,128]{2,1,0:T(8,128)S(1)} %constant_dynamic-slice_fusion.1, f32[16,256]{0,1:T(8,128)S(1)} %copy.61), kind=kLoop, calls=%fused_computation.35 | loop fusion | flops 1572864 | bytes 6307840 | tf_op jit(solution)/shard_map/div | solution.py:95
  325.4 2.0 copy.62
  (75 shorter events, 2.1 us)
Async XLA Ops:
  31.5 2.0 copy-start.4
  35.5 26.6 %all-to-all-start = ((bf16[16,256,128]{2,1,0:T(8,128)(2,1)}), bf16[16,256,128]{2,1,0:T(8,128)(2,1)S(1)}, u32[]{:S(2)}, u32[]{:S(2)}) async-start(bf16[16,256,128]{2,1,0:T(8,128)(2,1)} %gather_fusion.1), calls=%async_computation | async-start | bytes 2097152 | tf_op jit(solution)/shard_map/all_to_all | solution.py:49
  39.1 4.2 %copy-start.5 = (bf16[16384,128]{1,0:T(8,128)(2,1)S(1)}, bf16[16384,128]{1,0:T(8,128)(2,1)}, u32[]{:S(2)}) copy-start(bf16[16384,128]{1,0:T(8,128)(2,1)} %param.5) | copy-start | bytes 12582916
  62.0 1.8 copy-start
  83.1 5.0 %copy-start.2 = (f32[16,256,128]{2,0,1:T(8,128)S(1)}, f32[16,256,128]{2,0,1:T(8,128)}, u32[]{:S(2)}) copy-start(f32[16,256,128]{2,0,1:T(8,128)} %get-tuple-element.172) | copy-start | bytes 6291460 | tf_op jit(solution)/shard_map/while
  88.1 7.6 %copy-start.1 = (bf16[16,256,128]{2,1,0:T(8,128)(2,1)S(1)}, bf16[16,256,128]{2,1,0:T(8,128)(2,1)}, u32[]{:S(2)}) copy-start(bf16[16,256,128]{2,1,0:T(8,128)(2,1)} %copy-done) | copy-start | bytes 3145732 | tf_op jit(solution)/shard_map/while
  94.4 1.3 copy-start.3
  95.7 1.8 copy-start
  116.8 5.0 %copy-start.2 = (f32[16,256,128]{2,0,1:T(8,128)S(1)}, f32[16,256,128]{2,0,1:T(8,128)}, u32[]{:S(2)}) copy-start(f32[16,256,128]{2,0,1:T(8,128)} %get-tuple-element.172) | copy-start | bytes 6291460 | tf_op jit(solution)/shard_map/while
  121.8 7.6 %copy-start.1 = (bf16[16,256,128]{2,1,0:T(8,128)(2,1)S(1)}, bf16[16,256,128]{2,1,0:T(8,128)(2,1)}, u32[]{:S(2)}) copy-start(bf16[16,256,128]{2,1,0:T(8,128)(2,1)} %copy-done) | copy-start | bytes 3145732 | tf_op jit(solution)/shard_map/while
  128.1 1.3 copy-start.3
  129.4 1.8 copy-start
  150.5 5.0 %copy-start.2 = (f32[16,256,128]{2,0,1:T(8,128)S(1)}, f32[16,256,128]{2,0,1:T(8,128)}, u32[]{:S(2)}) copy-start(f32[16,256,128]{2,0,1:T(8,128)} %get-tuple-element.172) | copy-start | bytes 6291460 | tf_op jit(solution)/shard_map/while
  155.5 7.6 %copy-start.1 = (bf16[16,256,128]{2,1,0:T(8,128)(2,1)S(1)}, bf16[16,256,128]{2,1,0:T(8,128)(2,1)}, u32[]{:S(2)}) copy-start(bf16[16,256,128]{2,1,0:T(8,128)(2,1)} %copy-done) | copy-start | bytes 3145732 | tf_op jit(solution)/shard_map/while
  161.8 1.3 copy-start.3
  163.1 1.8 copy-start
  184.2 5.0 %copy-start.2 = (f32[16,256,128]{2,0,1:T(8,128)S(1)}, f32[16,256,128]{2,0,1:T(8,128)}, u32[]{:S(2)}) copy-start(f32[16,256,128]{2,0,1:T(8,128)} %get-tuple-element.172) | copy-start | bytes 6291460 | tf_op jit(solution)/shard_map/while
  189.2 7.6 %copy-start.1 = (bf16[16,256,128]{2,1,0:T(8,128)(2,1)S(1)}, bf16[16,256,128]{2,1,0:T(8,128)(2,1)}, u32[]{:S(2)}) copy-start(bf16[16,256,128]{2,1,0:T(8,128)(2,1)} %copy-done) | copy-start | bytes 3145732 | tf_op jit(solution)/shard_map/while
  195.5 1.3 copy-start.3
  197.4 13.3 %all-to-all-start.2 = ((f32[16,1,256]{2,1,0:T(1,128)}), f32[16,1,256]{2,1,0:T(1,128)S(1)}, u32[]{:S(2)}, u32[]{:S(2)}) async-start(f32[16,1,256]{2,1,0:T(1,128)} %all_to_all.16), calls=%async_computation.3 | async-start | bytes 32768 | tf_op jit(solution)/shard_map/all_to_all | solution.py:90
  210.8 44.8 %all-to-all-start.1 = ((f32[16,256,128]{2,1,0:T(8,128)}), f32[16,256,128]{2,1,0:T(8,128)S(1)}, u32[]{:S(2)}, u32[]{:S(2)}) async-start(f32[16,256,128]{2,1,0:T(8,128)} %copy.58), calls=%async_computation.1 | async-start | bytes 4194304 | tf_op jit(solution)/shard_map/all_to_all | solution.py:89
  214.5 47.8 %reduce-scatter.5.cloned.1.call-start = ((), (), s32[]{:S(2)}) async-start(), calls=%async_computation.6 | async-start | bytes 49152 | tf_op jit(solution)/shard_map/reduce_scatter | solution.py:28
  215.4 106.1 %reduce-scatter.3.cloned.1.call-start = ((), (), s32[]{:S(2)}) async-start(), calls=%async_computation.5 | async-start | bytes 6291456 | tf_op jit(solution)/shard_map/reduce_scatter | solution.py:27
Sparse Core Ops, SparseCore 0:
  218.1 11.1 reduce-scatter.4
  260.6 60.8 reduce-scatter.2
where the time goes:
time: 336 us; the launch traced here: 334 us
  waiting for transfers between devices  111 us (33%)
  local copies, waits for them, and re-layouts  67.3 us (20%)
  matrix products  64.7 us (19%)
  other arithmetic  45.1 us (13%)
  between operations  14.9 us (4%)
  starting transfers between devices  14.3 us (4%)
  blocking collectives  13.9 us (4%)
    reduce_scatter x1, waiting for transfers between devices, finish_sums(): lax.psum_scatter(own_sums, 'slab', scatter_dimension=0, tiled=True)  57.1 us
    all_to_all x1, waiting for transfers between devices, shards(): lax.all_to_all(sum_acc, 'blk', split_axis=0, concat_axis=0, tiled=True)  40 us
    convert_element_type x4, local copies, waits for them, and re-layouts, accumulate(): weights.astype(jnp.bfloat16).reshape(group_size, TOK_BLK, 3, CENT_BLK)  34.5 us
    dot_general x4, matrix products, accumulate(): jnp.einsum('ns,ncd->scd', one_hot, partial_value.reshape(-1, CENT_BLK, EM...  25 us
    dot_general x4, matrix products, accumulate(): jnp.einsum('gtkc,gtd->gkcd', weights_low, token_rows, preferred_element_t...  19.9 us
    reduce_sum x4, other arithmetic, accumulate(): jnp.sum(weights.reshape(group_size, TOK_BLK, 3, CENT_BLK), axis=1)  19.8 us
    unnamed x1, blocking collectives  13.9 us
    dot_general x4, matrix products, accumulate(): jnp.einsum('wsy,way->wsa', token_rows, candidate_centroids, preferred_ele...  13.4 us
  transfers between devices with their start and end apart: 5, of which 4 were waited for; matrix products, arithmetic and copies ran while one was open for 8% of the time, Pallas kernels for 0%

commit v1 on v0

v1 whole, which is shorter than its diff:
```python
import functools
import math

import jax
import jax.numpy as jnp
from jax import lax
from jax.experimental import pallas as pl
from jax.experimental.pallas import tpu as pltpu
from jax.sharding import PartitionSpec as P

CENT_BLK = 256
TOK_BLK = 256
SOFTMAX_TEMP = 0.1
PRIOR_WEIGHT = 4.0
EPSILON = 1e-06
LEVELS = 32767.0
MESH = pl.DeviceIdType.MESH


def unit_rows(values):
    widened = values.astype(jnp.float32)
    return widened * lax.rsqrt(jnp.mean(widened * widened, axis=-1, keepdims=True) + EPSILON)


def greet(peers):
    barrier = pltpu.get_barrier_semaphore()
    for peer in peers:
        pl.semaphore_signal(barrier, inc=1, device_id=peer, device_id_type=MESH)
    pl.semaphore_wait(barrier, len(peers))


def fetch_kernel(owners, listed_ref, cent_ref, out_ref, req_ref, asked_v, asked_s, reply,
                 ask_send, ask_recv, ask_local, rep_send, rep_recv, own_sem):
    me = lax.axis_index("blk")
    slab = lax.axis_index("slab")
    per_owner = cent_ref.shape[0]

    lanes = lax.broadcasted_iota(jnp.int32, (listed_ref.shape[0], 128), 1)
    best = jnp.zeros((1, 128), jnp.int32)
    for j in range(listed_ref.shape[1]):
        inner = listed_ref[:, j : j + 1] - lanes * per_owner
        held = jnp.where((inner >= 0) & (inner < per_owner), inner + 1, 0)
        best = jnp.maximum(best, jnp.max(held, axis=0, keepdims=True))
    req_ref[...] = jnp.broadcast_to(best, req_ref.shape)

    greet([(lax.rem(me + off, owners), slab) for off in range(1, owners)])

    def ask(off):
        return pltpu.make_async_remote_copy(
            src_ref=req_ref, dst_ref=asked_v.at[me], send_sem=ask_send.at[off], recv_sem=ask_recv.at[off],
            device_id=(lax.rem(me + off, owners), slab), device_id_type=MESH)

    def asked_by(off):
        src = lax.rem(me - off + owners, owners)
        return pltpu.make_async_remote_copy(
            src_ref=req_ref, dst_ref=asked_v.at[src], send_sem=ask_send.at[off], recv_sem=ask_recv.at[off],
            device_id=(src, slab), device_id_type=MESH)

    def give(off):
        return pltpu.make_async_remote_copy(
            src_ref=reply.at[off], dst_ref=out_ref.at[me], send_sem=rep_send.at[off], recv_sem=rep_recv.at[off],
            device_id=(lax.rem(me - off + owners, owners), slab), device_id_type=MESH)

    def given_by(off):
        src = lax.rem(me + off, owners)
        return pltpu.make_async_remote_copy(
            src_ref=reply.at[off], dst_ref=out_ref.at[src], send_sem=rep_send.at[off], recv_sem=rep_recv.at[off],
            device_id=(src, slab), device_id_type=MESH)

    def answer(off, source, src):
        pull = pltpu.make_async_copy(source, asked_s.at[src], ask_local)
        pull.start()
        pull.wait()
        wanted = jnp.maximum(asked_s[src, 0, me] - 1, 0)
        reply[off] = unit_rows(cent_ref[wanted]).astype(jnp.bfloat16)

    @pl.loop(1, owners)
    def _(off):
        ask(off).start()

    answer(0, req_ref, me)
    own = pltpu.make_async_copy(reply.at[0], out_ref.at[me], own_sem)
    own.start()

    @pl.loop(1, owners)
    def _(off):
        src = lax.rem(me - off + owners, owners)
        asked_by(off).wait_recv()
        answer(off, asked_v.at[src], src)
        give(off).start()

    own.wait()

    @pl.loop(1, owners)
    def _(off):
        ask(off).wait_send()
        give(off).wait_send()
        given_by(off).wait_recv()


def softmax_kernel(group, slots_ref, req_ref, tok_ref, cent_ref, q_ref, meta_ref, total, mass):
    step = pl.program_id(0)
    owners = cent_ref.shape[0]
    width = tok_ref.shape[-1]
    factor = math.log2(math.e) / (width * SOFTMAX_TEMP)

    @pl.when(step == 0)
    def _():
        total[...] = jnp.zeros_like(total)
        mass[...] = jnp.zeros_like(mass)

    for g in range(group):
        tok = unit_rows(tok_ref[g]).astype(jnp.bfloat16)
        slots = [slots_ref[(step * group + g) * 3 + j] for j in range(3)]
        grown = []
        norm = jnp.zeros((1, TOK_BLK), jnp.float32)
        for slot in slots:
            scores = lax.dot_general(cent_ref[slot], tok, (((1,), (1,)), ((), ())),
                                     preferred_element_type=jnp.float32)
            grown.append(jnp.exp2(scores * factor))
            norm = norm + jnp.sum(grown[-1], axis=0, keepdims=True)
        scale = 1.0 / norm
        for slot, value in zip(slots, grown):
            weights = value * scale
            part = weights[:, :128]
            for lane in range(128, TOK_BLK, 128):
                part = part + weights[:, lane : lane + 128]
            mass[slot] += part
            total[slot] += jnp.dot(weights.astype(jnp.bfloat16), tok, preferred_element_type=jnp.float32)

    @pl.when(step == pl.num_programs(0) - 1)
    def _():
        lanes = lax.broadcasted_iota(jnp.int32, (CENT_BLK, 128), 1)
        table = jnp.zeros((CENT_BLK, 128), jnp.float32)
        for k in range(owners):
            sums = total[k]
            top = jnp.max(jnp.abs(sums), axis=1, keepdims=True)
            inverse = LEVELS / jnp.maximum(top, 1e-30)
            q_ref[k] = jnp.floor(sums * inverse + 0.5).astype(jnp.int32).astype(jnp.int16)
            count = jnp.sum(mass[k], axis=1, keepdims=True)
            wanted = jnp.maximum(req_ref[k] - 1, 0).astype(jnp.float32)
            table = jnp.where(lanes == k, top * (1.0 / LEVELS), table)
            table = jnp.where(lanes == owners + k, count, table)
            table = jnp.where(lanes == 2 * owners + k, wanted, table)
        turned = table.T
        for kind in range(3):
            meta_ref[:, kind, :] = turned[kind * owners : (kind + 1) * owners]
        for kind in range(3, 8):
            meta_ref[:, kind, :] = jnp.zeros((owners, CENT_BLK), jnp.float32)


def return_kernel(owners, slabs, q_ref, meta_ref, q_out, meta_out, send_sem, recv_sem, fwd_send, fwd_recv, own_sem):
    me = lax.axis_index("blk")
    slab = lax.axis_index("slab")
    greet([(lax.rem(me + off, owners), slab) for off in range(1, owners)]
          + [(me, lax.rem(slab + t, slabs)) for t in range(1, slabs)])
    pairs = ((q_ref, q_out), (meta_ref, meta_out))

    def give(kind, off):
        dest = lax.rem(me + off, owners)
        source, target = pairs[kind]
        return pltpu.make_async_remote_copy(
            src_ref=source.at[dest], dst_ref=target.at[slab, me], send_sem=send_sem.at[kind, off],
            recv_sem=recv_sem.at[kind, off], device_id=(dest, slab), device_id_type=MESH)

    def given(kind, off):
        src = lax.rem(me - off + owners, owners)
        source, target = pairs[kind]
        return pltpu.make_async_remote_copy(
            src_ref=source.at[src], dst_ref=target.at[slab, src], send_sem=send_sem.at[kind, off],
            recv_sem=recv_sem.at[kind, off], device_id=(src, slab), device_id_type=MESH)

    def forward(kind, off, t):
        src = lax.rem(me - off + owners, owners)
        target = pairs[kind][1]
        return pltpu.make_async_remote_copy(
            src_ref=target.at[slab, src], dst_ref=target.at[slab, src], send_sem=fwd_send.at[kind, t, off],
            recv_sem=fwd_recv.at[kind, t, off], device_id=(me, lax.rem(slab + t, slabs)), device_id_type=MESH)

    def forwarded(kind, off, t):
        src = lax.rem(me - off + owners, owners)
        peer = lax.rem(slab - t + slabs, slabs)
        target = pairs[kind][1]
        return pltpu.make_async_remote_copy(
            src_ref=target.at[peer, src], dst_ref=target.at[peer, src], send_sem=fwd_send.at[kind, t, off],
            recv_sem=fwd_recv.at[kind, t, off], device_id=(me, peer), device_id_type=MESH)

    @pl.loop(1, owners)
    def _(off):
        for kind in range(2):
            give(kind, off).start()

    for kind in range(2):
        source, target = pairs[kind]
        own = pltpu.make_async_copy(source.at[me], target.at[slab, me], own_sem.at[kind])
        own.start()
        own.wait()
        for t in range(1, slabs):
            forward(kind, 0, t).start()

    @pl.loop(1, owners)
    def _(off):
        for kind in range(2):
            given(kind, off).wait_recv()
            for t in range(1, slabs):
                forward(kind, off, t).start()

    @pl.loop(1, owners)
    def _(off):
        for kind in range(2):
            give(kind, off).wait_send()

    @pl.loop(0, owners)
    def _(off):
        for kind in range(2):
            for t in range(1, slabs):
                forward(kind, off, t).wait_send()
                forwarded(kind, off, t).wait_recv()


def finish_kernel(ids_ref, q_ref, meta_ref, cent_ref, out_ref, count_ref):
    contributions = q_ref.shape[0]
    share = cent_ref.shape[0]
    first = ids_ref[contributions] * share
    out_ref[...] = PRIOR_WEIGHT * unit_rows(cent_ref[...])
    count_ref[...] = jnp.zeros_like(count_ref)
    for start in range(0, contributions, 128):
        many = min(128, contributions - start)
        rows = meta_ref[start : start + many, 0, :]
        if many < 128:
            rows = jnp.concatenate([rows, jnp.zeros((128 - many, CENT_BLK), jnp.float32)], axis=0)
        scales = rows.T
        for k in range(many):
            inner = ids_ref[start + k] - first

            @pl.when((inner >= 0) & (inner < share))
            def _():
                out_ref[inner] += q_ref[start + k].astype(jnp.float32) * scales[:, k : k + 1]
                count_ref[pl.ds(inner, 1), :] += meta_ref[start + k, 1:2, :]

    masses = jnp.concatenate([count_ref[...], jnp.zeros((128 - share, CENT_BLK), jnp.float32)], axis=0).T
    for i in range(share):
        out_ref[i] = out_ref[i] / (masses[:, i : i + 1] + PRIOR_WEIGHT)


def shards(owners, slabs, tokens, listed, centroids):
    width = tokens.shape[-1]
    blocks = listed.shape[0]
    per_owner = centroids.shape[0] // CENT_BLK
    share = per_owner // slabs
    cents = centroids.reshape(per_owner, CENT_BLK, width)
    vmem = pl.BlockSpec(memory_space=pltpu.VMEM)
    anywhere = pl.BlockSpec(memory_space=pl.ANY)
    dma = pltpu.SemaphoreType.DMA

    fetched, req = pl.pallas_call(
        functools.partial(fetch_kernel, owners),
        out_shape=(jax.ShapeDtypeStruct((owners, CENT_BLK, width), jnp.bfloat16),
                   jax.ShapeDtypeStruct((8, 128), jnp.int32)),
        in_specs=[vmem, vmem],
        out_specs=(anywhere, vmem),
        scratch_shapes=[
            pltpu.VMEM((owners, 8, 128), jnp.int32),
            pltpu.SMEM((owners, 8, 128), jnp.int32),
            pltpu.VMEM((owners, CENT_BLK, width), jnp.bfloat16),
            dma((owners,)), dma((owners,)), dma, dma((owners,)), dma((owners,)), dma,
        ],
        compiler_params=pltpu.CompilerParams(
            collective_id=0, has_side_effects=True, vmem_limit_bytes=16 * 2**20),
        name="fetch",
    )(listed, cents)

    group = 2
    packed, meta = pl.pallas_call(
        functools.partial(softmax_kernel, group),
        out_shape=(jax.ShapeDtypeStruct((owners, CENT_BLK, width), jnp.int16),
                   jax.ShapeDtypeStruct((owners, 8, CENT_BLK), jnp.float32)),
        grid_spec=pltpu.PrefetchScalarGridSpec(
            num_scalar_prefetch=2,
            grid=(blocks // group,),
            in_specs=[
                pl.BlockSpec((group, TOK_BLK, width), lambda i, *_: (i, 0, 0)),
                pl.BlockSpec((owners, CENT_BLK, width), lambda i, *_: (0, 0, 0)),
            ],
            out_specs=[
                pl.BlockSpec((owners, CENT_BLK, width), lambda i, *_: (0, 0, 0)),
                pl.BlockSpec((owners, 8, CENT_BLK), lambda i, *_: (0, 0, 0)),
            ],
            scratch_shapes=[
                pltpu.VMEM((owners, CENT_BLK, width), jnp.float32),
                pltpu.VMEM((owners, CENT_BLK, 128), jnp.float32),
            ],
        ),
        compiler_params=pltpu.CompilerParams(
            dimension_semantics=("arbitrary",), vmem_limit_bytes=40 * 2**20),
        name="softmax",
    )((listed // per_owner).reshape(-1), req[0], tokens.reshape(blocks, TOK_BLK, width), fetched)

    q_all, meta_all = pl.pallas_call(
        functools.partial(return_kernel, owners, slabs),
        out_shape=(jax.ShapeDtypeStruct((slabs, owners, CENT_BLK, width), jnp.int16),
                   jax.ShapeDtypeStruct((slabs, owners, 8, CENT_BLK), jnp.float32)),
        in_specs=[anywhere, anywhere],
        out_specs=(anywhere, anywhere),
        scratch_shapes=[dma((2, owners)), dma((2, owners)), dma((2, slabs, owners)), dma((2, slabs, owners)), dma((2,))],
        compiler_params=pltpu.CompilerParams(collective_id=1, has_side_effects=True),
        name="give_back",
    )(packed, meta)

    contributions = slabs * owners
    meta_flat = meta_all.reshape(contributions, 8, CENT_BLK)
    ids = jnp.concatenate([meta_flat[:, 2, 0].astype(jnp.int32), lax.axis_index("slab").astype(jnp.int32)[None]])
    refined, counts = pl.pallas_call(
        finish_kernel,
        out_shape=(jax.ShapeDtypeStruct((share, CENT_BLK, width), jnp.float32),
                   jax.ShapeDtypeStruct((share, CENT_BLK), jnp.float32)),
        grid_spec=pltpu.PrefetchScalarGridSpec(
            num_scalar_prefetch=1,
            grid=(1,),
            in_specs=[
                pl.BlockSpec((contributions, CENT_BLK, width), lambda i, *_: (0, 0, 0)),
                pl.BlockSpec((contributions, 8, CENT_BLK), lambda i, *_: (0, 0, 0)),
                pl.BlockSpec((share, CENT_BLK, width), lambda i, ids: (ids[contributions], 0, 0)),
            ],
            out_specs=[
                pl.BlockSpec((share, CENT_BLK, width), lambda i, *_: (0, 0, 0)),
                pl.BlockSpec((share, CENT_BLK), lambda i, *_: (0, 0)),
            ],
        ),
        compiler_params=pltpu.CompilerParams(
            dimension_semantics=("arbitrary",), vmem_limit_bytes=56 * 2**20),
        name="finish",
    )(ids, q_all.reshape(contributions, CENT_BLK, width), meta_flat, cents)
    return refined.reshape(share * CENT_BLK, width), counts.reshape(share * CENT_BLK)


def solution(mesh):
    placed = (P(("blk", "slab"), None), P(("blk", "slab"), None), P("blk", None))
    return jax.shard_map(
        functools.partial(shards, mesh.shape["blk"], mesh.shape["slab"]),
        mesh=mesh,
        in_specs=placed,
        out_specs=(P(("blk", "slab"), None), P(("blk", "slab"))),
        check_vma=False,
    )
```

time: 336 us -> 136 us (0.40)
  the two profiles are of different devices: /device:TPU:0 before, /device:TPU:24 now
where the time goes in v1:
time: 136 us
  Pallas kernels  125 us (92%)
  local copies, waits for them, and re-layouts  7.72 us (6%)
  other arithmetic  2.86 us (2%)
    pallas_call x1, Pallas kernels, shards(): pl.pallas_call(functools.partial(return_kernel, owners, slabs), out_shape...  51.3 us
    pallas_call x1, Pallas kernels, shards(): pl.pallas_call(functools.partial(softmax_kernel, group), out_shape=(jax.S...  37.7 us
    pallas_call x1, Pallas kernels, shards(): pl.pallas_call(functools.partial(fetch_kernel, owners), out_shape=(jax.Sh...  28.1 us
    pallas_call x1, Pallas kernels, shards(): pl.pallas_call(finish_kernel, out_shape=(jax.ShapeDtypeStruct((share, CEN...  7.64 us
    unnamed x10, local copies, waits for them, and re-layouts  7.49 us

profile of v1, /device:TPU:24, one launch (start us, length us, event | category | flops | bytes accessed | tf_op | source)
XLA Modules:
  0.0 136.0 jit_solution(8269336079628581248)
XLA Ops:
  0.6 0.7 add_select_fusion
  1.3 0.1 copy.6
  1.4 0.1 reshape.26.slots_ref
  1.6 0.8 copy.7.listed_ref
  2.3 0.0 copy-start
  2.3 1.6 %copy-done = bf16[8192,128]{1,0:T(8,128)(2,1)S(1)} copy-done((bf16[8192,128]{1,0:T(8,128)(2,1)S(1)}, bf16[8192,128]{1,0:T(8,128)(2,1)}, u32[]{:S(2)}) %copy-start) | copy-done | bytes 2097176
  3.9 28.1 %fetch.1 = (bf16[16,256,128]{2,1,0:T(8,128)(2,1)S(1)}, s32[8,128]{1,0:T(8,128)S(1)}) custom-call(s32[64,3]{1,0:T(8,128)S(1)} %copy.7.listed_ref, bf16[32,256,128]{2,1,0:T(8,128)(2,1)S(1)} %bitcast.11), custom_call_target="tpu_custom_call" | custom-call | tf_op jit(solution)/shard_map/fetch/pallas_call | solution.py:256
  32.0 0.0 copy-start.1
  32.0 2.2 %copy-done.1 = bf16[16384,128]{1,0:T(8,128)(2,1)S(1)} copy-done((bf16[16384,128]{1,0:T(8,128)(2,1)S(1)}, bf16[16384,128]{1,0:T(8,128)(2,1)}, u32[]{:S(2)}) %copy-start.1) | copy-done | bytes 4194328
  34.2 37.7 %softmax.1 = (s16[16,256,128]{2,1,0:T(8,128)(2,1)S(1)}, f32[16,8,256]{2,1,0:T(8,128)S(1)}) custom-call(s32[192]{0:T(256)S(1)} %reshape.26.slots_ref, s32[128]{0:T(128)S(1)} %slice_bitcast_fusion.req_ref, bf16[64,256,128]{2,1,0:T(8,128)(2,1)S(1)} %bitcast.12, bf16[16,256,128]{2,1,0:T(8,128)(2,1)S(1)} %get-tuple-element.11.cent_ref), custom_call_target="tpu_custom_call" | custom-call | tf_op jit(solution)/shard_map/softmax/pallas_call | solution.py:274
  71.9 0.0 copy-start.2
  71.9 1.0 copy-done.2
  72.8 0.0 copy-start.3
  72.8 0.6 copy-done.3
  73.5 51.3 %give_back.1 = (s16[2,16,256,128]{3,2,1,0:T(8,128)(2,1)}, f32[2,16,8,256]{3,2,1,0:T(8,128)}) custom-call(s16[16,256,128]{2,1,0:T(8,128)(2,1)} %copy-done.2, f32[16,8,256]{2,1,0:T(8,128)} %copy-done.3), custom_call_target="tpu_custom_call" | custom-call | tf_op jit(solution)/shard_map/give_back/pallas_call | solution.py:299
  124.8 1.6 %fusion = s32[32]{0:T(128)S(1)} fusion(f32[32,8,256]{2,1,0:T(8,128)} %bitcast.14), kind=kLoop, calls=%fused_computation.1 | loop fusion | flops 32 | bytes 256 | tf_op jit(solution)/shard_map/convert_element_type | solution.py:312
  126.4 0.6 pad_add_fusion.ids_ref
  127.0 7.6 %finish.1 = (f32[16,256,128]{2,1,0:T(8,128)}, f32[16,256]{1,0:T(8,128)}) custom-call(s32[33]{0:T(128)} %pad_add_fusion.ids_ref, s16[32,256,128]{2,1,0:T(8,128)(2,1)} %bitcast.13, f32[32,8,256]{2,1,0:T(8,128)} %bitcast.15, bf16[32,256,128]{2,1,0:T(8,128)(2,1)} %bitcast.10), custom_call_target="tpu_custom_call" | custom-call | tf_op jit(solution)/shard_map/finish/pallas_call | solution.py:313
  134.6 1.3 copy.8
  (1 shorter events, 0.0 us)
Async XLA Ops:
  2.3 1.6 %copy-start = (bf16[8192,128]{1,0:T(8,128)(2,1)S(1)}, bf16[8192,128]{1,0:T(8,128)(2,1)}, u32[]{:S(2)}) copy-start(bf16[8192,128]{1,0:T(8,128)(2,1)} %param.5) | copy-start | bytes 6291460
  32.0 2.2 %copy-start.1 = (bf16[16384,128]{1,0:T(8,128)(2,1)S(1)}, bf16[16384,128]{1,0:T(8,128)(2,1)}, u32[]{:S(2)}) copy-start(bf16[16384,128]{1,0:T(8,128)(2,1)} %param.3) | copy-start | bytes 12582916
  71.9 1.0 copy-start.2
  72.8 0.6 copy-start.3

commit v2 on v1

--- a/solution.py
+++ b/solution.py
@@ -22,6 +22,17 @@
     return widened * lax.rsqrt(jnp.mean(widened * widened, axis=-1, keepdims=True) + EPSILON)
 
 
+def partner(me, off, count):
+    assert count & (count - 1) == 0
+    other = 0
+    bit = 1
+    while bit < count:
+        mine = lax.rem(me // bit, 2)
+        other = other + bit * (1 - mine if off & bit else mine)
+        bit *= 2
+    return other
+
+
 def greet(peers):
     barrier = pltpu.get_barrier_semaphore()
     for peer in peers:
@@ -43,15 +54,15 @@
         best = jnp.maximum(best, jnp.max(held, axis=0, keepdims=True))
     req_ref[...] = jnp.broadcast_to(best, req_ref.shape)
 
-    greet([(lax.rem(me + off, owners), slab) for off in range(1, owners)])
+    greet([(partner(me, off, owners), slab) for off in range(1, owners)])
 
     def ask(off):
         return pltpu.make_async_remote_copy(
             src_ref=req_ref, dst_ref=asked_v.at[me], send_sem=ask_send.at[off], recv_sem=ask_recv.at[off],
-            device_id=(lax.rem(me + off, owners), slab), device_id_type=MESH)
+            device_id=(partner(me, off, owners), slab), device_id_type=MESH)
 
     def asked_by(off):
-        src = lax.rem(me - off + owners, owners)
+        src = partner(me, off, owners)
         return pltpu.make_async_remote_copy(
             src_ref=req_ref, dst_ref=asked_v.at[src], send_sem=ask_send.at[off], recv_sem=ask_recv.at[off],
             device_id=(src, slab), device_id_type=MESH)
@@ -59,46 +70,36 @@
     def give(off):
         return pltpu.make_async_remote_copy(
             src_ref=reply.at[off], dst_ref=out_ref.at[me], send_sem=rep_send.at[off], recv_sem=rep_recv.at[off],
-            device_id=(lax.rem(me - off + owners, owners), slab), device_id_type=MESH)
+            device_id=(partner(me, off, owners), slab), device_id_type=MESH)
 
     def given_by(off):
-        src = lax.rem(me + off, owners)
+        src = partner(me, off, owners)
         return pltpu.make_async_remote_copy(
             src_ref=reply.at[off], dst_ref=out_ref.at[src], send_sem=rep_send.at[off], recv_sem=rep_recv.at[off],
             device_id=(src, slab), device_id_type=MESH)
 
-    def answer(off, source, src):
-        pull = pltpu.make_async_copy(source, asked_s.at[src], ask_local)
-        pull.start()
-        pull.wait()
-        wanted = jnp.maximum(asked_s[src, 0, me] - 1, 0)
+    far_first = list(range(owners - 1, 0, -1))
+    for off in far_first:
+        ask(off).start()
+    asked_v[me] = req_ref[...]
+    for off in far_first:
+        asked_by(off).wait_recv()
+    pull = pltpu.make_async_copy(asked_v.at[:, 0], asked_s, ask_local)
+    pull.start()
+    pull.wait()
+    own = pltpu.make_async_copy(reply.at[0], out_ref.at[me], own_sem)
+    for off in far_first + [0]:
+        wanted = jnp.maximum(asked_s[partner(me, off, owners), me] - 1, 0)
         reply[off] = unit_rows(cent_ref[wanted]).astype(jnp.bfloat16)
-
-    @pl.loop(1, owners)
-    def _(off):
-        ask(off).start()
-
-    answer(0, req_ref, me)
-    own = pltpu.make_async_copy(reply.at[0], out_ref.at[me], own_sem)
-    own.start()
-
-    @pl.loop(1, owners)
-    def _(off):
-        src = lax.rem(me - off + owners, owners)
-        asked_by(off).wait_recv()
-        answer(off, asked_v.at[src], src)
-        give(off).start()
-
+        (give(off) if off else own).start()
     own.wait()
-
-    @pl.loop(1, owners)
-    def _(off):
+    for off in far_first:
         ask(off).wait_send()
         give(off).wait_send()
         given_by(off).wait_recv()
 
 
-def softmax_kernel(group, slots_ref, req_ref, tok_ref, cent_ref, q_ref, meta_ref, total, mass):
+def softmax_kernel(group, slots_ref, req_ref, tok_ref, cent_ref, q_ref, meta_ref, total, mass, grown, tok_held, scales):
     step = pl.program_id(0)
     owners = cent_ref.shape[0]
     width = tok_ref.shape[-1]
@@ -108,28 +109,42 @@
     def _():
         total[...] = jnp.zeros_like(total)
         mass[...] = jnp.zeros_like(mass)
-
-    for g in range(group):
-        tok = unit_rows(tok_ref[g]).astype(jnp.bfloat16)
-        slots = [slots_ref[(step * group + g) * 3 + j] for j in range(3)]
-        grown = []
-        norm = jnp.zeros((1, TOK_BLK), jnp.float32)
-        for slot in slots:
-            scores = lax.dot_general(cent_ref[slot], tok, (((1,), (1,)), ((), ())),
-                                     preferred_element_type=jnp.float32)
-            grown.append(jnp.exp2(scores * factor))
-            norm = norm + jnp.sum(grown[-1], axis=0, keepdims=True)
-        scale = 1.0 / norm
-        for slot, value in zip(slots, grown):
-            weights = value * scale
+        grown[1] = jnp.zeros_like(grown[1])
+        tok_held[1] = jnp.zeros_like(tok_held[1])
+        scales[1] = jnp.zeros_like(scales[1])
+
+    def collect(block, side):
+        tok = tok_held[side]
+        scale = scales[side, 0:1]
+        for j in range(3):
+            slot = slots_ref[block * 3 + j]
+            weights = grown[side, j] * scale
             part = weights[:, :128]
             for lane in range(128, TOK_BLK, 128):
                 part = part + weights[:, lane : lane + 128]
             mass[slot] += part
             total[slot] += jnp.dot(weights.astype(jnp.bfloat16), tok, preferred_element_type=jnp.float32)
 
+    def grow(block, g, side):
+        tok = unit_rows(tok_ref[g]).astype(jnp.bfloat16)
+        tok_held[side] = tok
+        norm = jnp.zeros((1, TOK_BLK), jnp.float32)
+        for j in range(3):
+            scores = lax.dot_general(cent_ref[slots_ref[block * 3 + j]], tok, (((1,), (1,)), ((), ())),
+                                     preferred_element_type=jnp.float32)
+            value = jnp.exp2(scores * factor)
+            grown[side, j] = value
+            norm = norm + jnp.sum(value, axis=0, keepdims=True)
+        scales[side] = jnp.broadcast_to(1.0 / norm, (8, TOK_BLK))
+
+    for g in range(group):
+        block = step * group + g
+        collect(jnp.maximum(block - 1, 0), (g + 1) % 2)
+        grow(block, g, g % 2)
+
     @pl.when(step == pl.num_programs(0) - 1)
     def _():
+        collect(step * group + group - 1, (group + 1) % 2)
         lanes = lax.broadcasted_iota(jnp.int32, (CENT_BLK, 128), 1)
         table = jnp.zeros((CENT_BLK, 128), jnp.float32)
         for k in range(owners):
@@ -144,75 +159,71 @@
             table = jnp.where(lanes == 2 * owners + k, wanted, table)
         turned = table.T
         for kind in range(3):
-            meta_ref[:, kind, :] = turned[kind * owners : (kind + 1) * owners]
-        for kind in range(3, 8):
-            meta_ref[:, kind, :] = jnp.zeros((owners, CENT_BLK), jnp.float32)
+            rows = turned[kind * owners : (kind + 1) * owners]
+            for half in range(CENT_BLK // 128):
+                meta_ref[:, 2 * kind + half, :] = rows[:, half * 128 : (half + 1) * 128]
+        meta_ref[:, 6:, :] = jnp.zeros((owners, 2, 128), jnp.float32)
 
 
 def return_kernel(owners, slabs, q_ref, meta_ref, q_out, meta_out, send_sem, recv_sem, fwd_send, fwd_recv, own_sem):
     me = lax.axis_index("blk")
     slab = lax.axis_index("slab")
-    greet([(lax.rem(me + off, owners), slab) for off in range(1, owners)]
+    greet([(partner(me, off, owners), slab) for off in range(1, owners)]
           + [(me, lax.rem(slab + t, slabs)) for t in range(1, slabs)])
     pairs = ((q_ref, q_out), (meta_ref, meta_out))
 
     def give(kind, off):
-        dest = lax.rem(me + off, owners)
+        dest = partner(me, off, owners)
         source, target = pairs[kind]
         return pltpu.make_async_remote_copy(
             src_ref=source.at[dest], dst_ref=target.at[slab, me], send_sem=send_sem.at[kind, off],
             recv_sem=recv_sem.at[kind, off], device_id=(dest, slab), device_id_type=MESH)
 
     def given(kind, off):
-        src = lax.rem(me - off + owners, owners)
+        src = partner(me, off, owners)
         source, target = pairs[kind]
         return pltpu.make_async_remote_copy(
             src_ref=source.at[src], dst_ref=target.at[slab, src], send_sem=send_sem.at[kind, off],
             recv_sem=recv_sem.at[kind, off], device_id=(src, slab), device_id_type=MESH)
 
     def forward(kind, off, t):
-        src = lax.rem(me - off + owners, owners)
-        target = pairs[kind][1]
-        return pltpu.make_async_remote_copy(
-            src_ref=target.at[slab, src], dst_ref=target.at[slab, src], send_sem=fwd_send.at[kind, t, off],
-            recv_sem=fwd_recv.at[kind, t, off], device_id=(me, lax.rem(slab + t, slabs)), device_id_type=MESH)
+        src = partner(me, off, owners)
+        source, target = pairs[kind]
+        return pltpu.make_async_remote_copy(
+            src_ref=target.at[slab, src] if off else source.at[me], dst_ref=target.at[slab, src],
+            send_sem=fwd_send.at[kind, t, off], recv_sem=fwd_recv.at[kind, t, off],
+            device_id=(me, lax.rem(slab + t, slabs)), device_id_type=MESH)
 
     def forwarded(kind, off, t):
-        src = lax.rem(me - off + owners, owners)
+        src = partner(me, off, owners)
         peer = lax.rem(slab - t + slabs, slabs)
         target = pairs[kind][1]
         return pltpu.make_async_remote_copy(
             src_ref=target.at[peer, src], dst_ref=target.at[peer, src], send_sem=fwd_send.at[kind, t, off],
             recv_sem=fwd_recv.at[kind, t, off], device_id=(me, peer), device_id_type=MESH)
 
-    @pl.loop(1, owners)
-    def _(off):
+    half = owners // 2
+    order = [off for near in range(half) for off in ((half + near, near) if near else (half,))]
+    own = [pltpu.make_async_copy(source.at[me], target.at[slab, me], own_sem.at[kind])
+           for kind, (source, target) in enumerate(pairs)]
+    for kind in range(2):
+        for t in range(1, slabs):
+            forward(kind, 0, t).start()
+    for off in order:
         for kind in range(2):
             give(kind, off).start()
-
     for kind in range(2):
-        source, target = pairs[kind]
-        own = pltpu.make_async_copy(source.at[me], target.at[slab, me], own_sem.at[kind])
-        own.start()
-        own.wait()
-        for t in range(1, slabs):
-            forward(kind, 0, t).start()
-
-    @pl.loop(1, owners)
-    def _(off):
+        own[kind].start()
+    for off in order:
         for kind in range(2):
             given(kind, off).wait_recv()
             for t in range(1, slabs):
                 forward(kind, off, t).start()
-
-    @pl.loop(1, owners)
-    def _(off):
-        for kind in range(2):
+    for kind in range(2):
+        own[kind].wait()
+        for off in order:
             give(kind, off).wait_send()
-
-    @pl.loop(0, owners)
-    def _(off):
-        for kind in range(2):
+        for off in [0] + order:
             for t in range(1, slabs):
                 forward(kind, off, t).wait_send()
                 forwarded(kind, off, t).wait_recv()
@@ -226,7 +237,7 @@
     count_ref[...] = jnp.zeros_like(count_ref)
     for start in range(0, contributions, 128):
         many = min(128, contributions - start)
-        rows = meta_ref[start : start + many, 0, :]
+        rows = jnp.concatenate([meta_ref[start : start + many, half, :] for half in range(CENT_BLK // 128)], axis=1)
         if many < 128:
             rows = jnp.concatenate([rows, jnp.zeros((128 - many, CENT_BLK), jnp.float32)], axis=0)
         scales = rows.T
@@ -236,7 +247,8 @@
             @pl.when((inner >= 0) & (inner < share))
             def _():
                 out_ref[inner] += q_ref[start + k].astype(jnp.float32) * scales[:, k : k + 1]
-                count_ref[pl.ds(inner, 1), :] += meta_ref[start + k, 1:2, :]
+                parts = [meta_ref[start + k, 2 + half : 3 + half, :] for half in range(CENT_BLK // 128)]
+                count_ref[pl.ds(inner, 1), :] += jnp.concatenate(parts, axis=1)
 
     masses = jnp.concatenate([count_ref[...], jnp.zeros((128 - share, CENT_BLK), jnp.float32)], axis=0).T
     for i in range(share):
@@ -261,7 +273,7 @@
         out_specs=(anywhere, vmem),
         scratch_shapes=[
             pltpu.VMEM((owners, 8, 128), jnp.int32),
-            pltpu.SMEM((owners, 8, 128), jnp.int32),
+            pltpu.SMEM((owners, 128), jnp.int32),
             pltpu.VMEM((owners, CENT_BLK, width), jnp.bfloat16),
             dma((owners,)), dma((owners,)), dma, dma((owners,)), dma((owners,)), dma,
         ],
@@ -270,11 +282,11 @@
         name="fetch",
     )(listed, cents)
 
-    group = 2
+    group = 4
     packed, meta = pl.pallas_call(
         functools.partial(softmax_kernel, group),
         out_shape=(jax.ShapeDtypeStruct((owners, CENT_BLK, width), jnp.int16),
-                   jax.ShapeDtypeStruct((owners, 8, CENT_BLK), jnp.float32)),
+                   jax.ShapeDtypeStruct((owners, 8, 128), jnp.float32)),
         grid_spec=pltpu.PrefetchScalarGridSpec(
             num_scalar_prefetch=2,
             grid=(blocks // group,),
@@ -284,11 +296,14 @@
             ],
             out_specs=[
                 pl.BlockSpec((owners, CENT_BLK, width), lambda i, *_: (0, 0, 0)),
-                pl.BlockSpec((owners, 8, CENT_BLK), lambda i, *_: (0, 0, 0)),
+                pl.BlockSpec((owners, 8, 128), lambda i, *_: (0, 0, 0)),
             ],
             scratch_shapes=[
                 pltpu.VMEM((owners, CENT_BLK, width), jnp.float32),
                 pltpu.VMEM((owners, CENT_BLK, 128), jnp.float32),
+                pltpu.VMEM((2, 3, CENT_BLK, TOK_BLK), jnp.float32),
+                pltpu.VMEM((2, TOK_BLK, width), jnp.bfloat16),
+                pltpu.VMEM((2, 8, TOK_BLK), jnp.float32),
             ],
         ),
         compiler_params=pltpu.CompilerParams(
@@ -299,7 +314,7 @@
     q_all, meta_all = pl.pallas_call(
         functools.partial(return_kernel, owners, slabs),
         out_shape=(jax.ShapeDtypeStruct((slabs, owners, CENT_BLK, width), jnp.int16),
-                   jax.ShapeDtypeStruct((slabs, owners, 8, CENT_BLK), jnp.float32)),
+                   jax.ShapeDtypeStruct((slabs, owners, 8, 128), jnp.float32)),
         in_specs=[anywhere, anywhere],
         out_specs=(anywhere, anywhere),
         scratch_shapes=[dma((2, owners)), dma((2, owners)), dma((2, slabs, owners)), dma((2, slabs, owners)), dma((2,))],
@@ -308,8 +323,8 @@
     )(packed, meta)
 
     contributions = slabs * owners
-    meta_flat = meta_all.reshape(contributions, 8, CENT_BLK)
-    ids = jnp.concatenate([meta_flat[:, 2, 0].astype(jnp.int32), lax.axis_index("slab").astype(jnp.int32)[None]])
+    meta_flat = meta_all.reshape(contributions, 8, 128)
+    ids = jnp.concatenate([meta_flat[:, 4, 0].astype(jnp.int32), lax.axis_index("slab").astype(jnp.int32)[None]])
     refined, counts = pl.pallas_call(
         finish_kernel,
         out_shape=(jax.ShapeDtypeStruct((share, CENT_BLK, width), jnp.float32),
@@ -319,7 +334,7 @@
             grid=(1,),
             in_specs=[
                 pl.BlockSpec((contributions, CENT_BLK, width), lambda i, *_: (0, 0, 0)),
-                pl.BlockSpec((contributions, 8, CENT_BLK), lambda i, *_: (0, 0, 0)),
+                pl.BlockSpec((contributions, 8, 128), lambda i, *_: (0, 0, 0)),
                 pl.BlockSpec((share, CENT_BLK, width), lambda i, ids: (ids[contributions], 0, 0)),
             ],
             out_specs=[

time: 136 us -> 125 us (0.919)
  the two profiles are of different devices: /device:TPU:24 before, /device:TPU:0 now
where the time goes in v2:
time: 125 us
  Pallas kernels  114 us (91%)
  local copies, waits for them, and re-layouts  7.7 us (6%)
  other arithmetic  2.88 us (2%)
    pallas_call x1, Pallas kernels, shards(): pl.pallas_call(functools.partial(return_kernel, owners, slabs), out_shape...  41.3 us
    pallas_call x1, Pallas kernels, shards(): pl.pallas_call(functools.partial(fetch_kernel, owners), out_shape=(jax.Sh...  36.1 us
    pallas_call x1, Pallas kernels, shards(): pl.pallas_call(functools.partial(softmax_kernel, group), out_shape=(jax.S...  28.9 us
    pallas_call x1, Pallas kernels, shards(): pl.pallas_call(finish_kernel, out_shape=(jax.ShapeDtypeStruct((share, CEN...  7.62 us
    unnamed x10, local copies, waits for them, and re-layouts  7.47 us

profile of v2, /device:TPU:0, one launch (start us, length us, event | category | flops | bytes accessed | tf_op | source)
XLA Modules:
  0.0 125.2 jit_solution(14531008927333401220)
XLA Ops:
  0.6 0.7 add_select_fusion
  1.3 0.1 copy.6
  1.4 0.1 reshape.26.slots_ref
  1.6 0.8 copy.7.listed_ref
  2.3 0.0 copy-start
  2.3 1.6 %copy-done = bf16[8192,128]{1,0:T(8,128)(2,1)S(1)} copy-done((bf16[8192,128]{1,0:T(8,128)(2,1)S(1)}, bf16[8192,128]{1,0:T(8,128)(2,1)}, u32[]{:S(2)}) %copy-start) | copy-done | bytes 2097176
  3.9 36.1 %fetch.1 = (bf16[16,256,128]{2,1,0:T(8,128)(2,1)S(1)}, s32[8,128]{1,0:T(8,128)S(1)}) custom-call(s32[64,3]{1,0:T(8,128)S(1)} %copy.7.listed_ref, bf16[32,256,128]{2,1,0:T(8,128)(2,1)S(1)} %bitcast.11), custom_call_target="tpu_custom_call" | custom-call | tf_op jit(solution)/shard_map/fetch/pallas_call | solution.py:268
  40.0 0.0 copy-start.1
  40.0 2.2 %copy-done.1 = bf16[16384,128]{1,0:T(8,128)(2,1)S(1)} copy-done((bf16[16384,128]{1,0:T(8,128)(2,1)S(1)}, bf16[16384,128]{1,0:T(8,128)(2,1)}, u32[]{:S(2)}) %copy-start.1) | copy-done | bytes 4194328
  42.2 28.9 %softmax.1 = (s16[16,256,128]{2,1,0:T(8,128)(2,1)S(1)}, f32[16,8,128]{2,1,0:T(8,128)S(1)}) custom-call(s32[192]{0:T(256)S(1)} %reshape.26.slots_ref, s32[128]{0:T(128)S(1)} %slice_bitcast_fusion.req_ref, bf16[64,256,128]{2,1,0:T(8,128)(2,1)S(1)} %bitcast.12, bf16[16,256,128]{2,1,0:T(8,128)(2,1)S(1)} %get-tuple-element.11.cent_ref), custom_call_target="tpu_custom_call" | custom-call | tf_op jit(solution)/shard_map/softmax/pallas_call | solution.py:286
  71.1 0.0 copy-start.2
  71.2 1.0 copy-done.2
  72.1 0.0 copy-start.3
  72.1 0.6 copy-done.3
  72.7 41.3 %give_back.1 = (s16[2,16,256,128]{3,2,1,0:T(8,128)(2,1)}, f32[2,16,8,128]{3,2,1,0:T(8,128)}) custom-call(s16[16,256,128]{2,1,0:T(8,128)(2,1)} %copy-done.2, f32[16,8,128]{2,1,0:T(8,128)} %copy-done.3), custom_call_target="tpu_custom_call" | custom-call | tf_op jit(solution)/shard_map/give_back/pallas_call | solution.py:314
  114.0 1.6 %fusion = s32[32]{0:T(128)S(1)} fusion(f32[32,8,128]{2,1,0:T(8,128)} %bitcast.14), kind=kLoop, calls=%fused_computation.1 | loop fusion | flops 32 | bytes 256 | tf_op jit(solution)/shard_map/convert_element_type | solution.py:327
  115.6 0.6 pad_add_fusion.ids_ref
  116.2 7.6 %finish.1 = (f32[16,256,128]{2,1,0:T(8,128)}, f32[16,256]{1,0:T(8,128)}) custom-call(s32[33]{0:T(128)} %pad_add_fusion.ids_ref, s16[32,256,128]{2,1,0:T(8,128)(2,1)} %bitcast.13, f32[32,8,128]{2,1,0:T(8,128)} %bitcast.15, bf16[32,256,128]{2,1,0:T(8,128)(2,1)} %bitcast.10), custom_call_target="tpu_custom_call" | custom-call | tf_op jit(solution)/shard_map/finish/pallas_call | solution.py:328
  123.8 1.3 %copy.8 = f32[2,2,8,128]{3,1,2,0:T(2,128)} copy(f32[2,2,8,128]{3,2,1,0:T(8,128)} %bitcast.16) | data formatting | bytes 32768
  (1 shorter events, 0.0 us)
Async XLA Ops:
  2.3 1.6 %copy-start = (bf16[8192,128]{1,0:T(8,128)(2,1)S(1)}, bf16[8192,128]{1,0:T(8,128)(2,1)}, u32[]{:S(2)}) copy-start(bf16[8192,128]{1,0:T(8,128)(2,1)} %param.5) | copy-start | bytes 6291460
  40.0 2.2 %copy-start.1 = (bf16[16384,128]{1,0:T(8,128)(2,1)S(1)}, bf16[16384,128]{1,0:T(8,128)(2,1)}, u32[]{:S(2)}) copy-start(bf16[16384,128]{1,0:T(8,128)(2,1)} %param.3) | copy-start | bytes 12582916
  71.1 1.0 copy-start.2
  72.1 0.6 copy-start.3

commit v3 on v2

--- a/solution.py
+++ b/solution.py
@@ -40,19 +40,21 @@
     pl.semaphore_wait(barrier, len(peers))
 
 
-def fetch_kernel(owners, listed_ref, cent_ref, out_ref, req_ref, asked_v, asked_s, reply,
+def fetch_kernel(owners, listed_ref, cent_ref, out_ref, req_ref, cents, asked_v, asked_s, reply, cent_sem,
                  ask_send, ask_recv, ask_local, rep_send, rep_recv, own_sem):
     me = lax.axis_index("blk")
     slab = lax.axis_index("slab")
     per_owner = cent_ref.shape[0]
 
-    lanes = lax.broadcasted_iota(jnp.int32, (listed_ref.shape[0], 128), 1)
-    best = jnp.zeros((1, 128), jnp.int32)
-    for j in range(listed_ref.shape[1]):
-        inner = listed_ref[:, j : j + 1] - lanes * per_owner
+    load = pltpu.make_async_copy(cent_ref, cents, cent_sem)
+    load.start()
+    rows = lax.broadcasted_iota(jnp.int32, (128, listed_ref.shape[1]), 0)
+    best = jnp.zeros((128, 1), jnp.int32)
+    for j in range(listed_ref.shape[0]):
+        inner = listed_ref[j : j + 1, :] - rows * per_owner
         held = jnp.where((inner >= 0) & (inner < per_owner), inner + 1, 0)
-        best = jnp.maximum(best, jnp.max(held, axis=0, keepdims=True))
-    req_ref[...] = jnp.broadcast_to(best, req_ref.shape)
+        best = jnp.maximum(best, jnp.max(held, axis=1, keepdims=True))
+    req_ref[...] = jnp.broadcast_to(best, (128, 128)).T[0:1]
 
     greet([(partner(me, off, owners), slab) for off in range(1, owners)])
 
@@ -88,9 +90,10 @@
     pull.start()
     pull.wait()
     own = pltpu.make_async_copy(reply.at[0], out_ref.at[me], own_sem)
+    load.wait()
     for off in far_first + [0]:
         wanted = jnp.maximum(asked_s[partner(me, off, owners), me] - 1, 0)
-        reply[off] = unit_rows(cent_ref[wanted]).astype(jnp.bfloat16)
+        reply[off] = unit_rows(cents[wanted]).astype(jnp.bfloat16)
         (give(off) if off else own).start()
     own.wait()
     for off in far_first:
@@ -99,7 +102,7 @@
         given_by(off).wait_recv()
 
 
-def softmax_kernel(group, slots_ref, req_ref, tok_ref, cent_ref, q_ref, meta_ref, total, mass, grown, tok_held, scales):
+def softmax_kernel(group, per_owner, listed_ref, req_ref, tok_ref, cent_ref, q_ref, meta_ref, total, mass, grown, tok_held, scales):
     step = pl.program_id(0)
     owners = cent_ref.shape[0]
     width = tok_ref.shape[-1]
@@ -117,7 +120,7 @@
         tok = tok_held[side]
         scale = scales[side, 0:1]
         for j in range(3):
-            slot = slots_ref[block * 3 + j]
+            slot = lax.div(listed_ref[j, block], per_owner)
             weights = grown[side, j] * scale
             part = weights[:, :128]
             for lane in range(128, TOK_BLK, 128):
@@ -130,7 +133,7 @@
         tok_held[side] = tok
         norm = jnp.zeros((1, TOK_BLK), jnp.float32)
         for j in range(3):
-            scores = lax.dot_general(cent_ref[slots_ref[block * 3 + j]], tok, (((1,), (1,)), ((), ())),
+            scores = lax.dot_general(cent_ref[lax.div(listed_ref[j, block], per_owner)], tok, (((1,), (1,)), ((), ())),
                                      preferred_element_type=jnp.float32)
             value = jnp.exp2(scores * factor)
             grown[side, j] = value
@@ -153,7 +156,7 @@
             inverse = LEVELS / jnp.maximum(top, 1e-30)
             q_ref[k] = jnp.floor(sums * inverse + 0.5).astype(jnp.int32).astype(jnp.int16)
             count = jnp.sum(mass[k], axis=1, keepdims=True)
-            wanted = jnp.maximum(req_ref[k] - 1, 0).astype(jnp.float32)
+            wanted = jnp.maximum(req_ref[0, k] - 1, 0).astype(jnp.float32)
             table = jnp.where(lanes == k, top * (1.0 / LEVELS), table)
             table = jnp.where(lanes == owners + k, count, table)
             table = jnp.where(lanes == 2 * owners + k, wanted, table)
@@ -203,38 +206,62 @@
             recv_sem=fwd_recv.at[kind, t, off], device_id=(me, peer), device_id_type=MESH)
 
     half = owners // 2
-    order = [off for near in range(half) for off in ((half + near, near) if near else (half,))]
+    near, far = list(range(1, half)), list(range(half, owners))
     own = [pltpu.make_async_copy(source.at[me], target.at[slab, me], own_sem.at[kind])
            for kind, (source, target) in enumerate(pairs)]
-    for kind in range(2):
-        for t in range(1, slabs):
-            forward(kind, 0, t).start()
-    for off in order:
+
+    def send(off):
+        for kind in (1, 0):
+            give(kind, off).start()
+
+    def pass_on(off):
         for kind in range(2):
-            give(kind, off).start()
+            if off:
+                given(kind, off).wait_recv()
+            for t in range(1, slabs):
+                forward(kind, off, t).start()
+
+    pass_on(0)
+    send(far[0])
+    for off in near:
+        send(off)
+    send(far[1])
     for kind in range(2):
         own[kind].start()
-    for off in order:
+    ready = list(near)
+    for i, off in enumerate(far):
+        pass_on_now, ready = ready[:2], ready[2:]
+        for other in pass_on_now:
+            pass_on(other)
         for kind in range(2):
-            given(kind, off).wait_recv()
-            for t in range(1, slabs):
-                forward(kind, off, t).start()
+            give(kind, off).wait_send()
+        if i + 2 < len(far):
+            send(far[i + 2])
+        ready.append(off)
+    for off in ready:
+        pass_on(off)
     for kind in range(2):
         own[kind].wait()
-        for off in order:
+        for off in near:
             give(kind, off).wait_send()
-        for off in [0] + order:
+        for off in [0] + near + far:
             for t in range(1, slabs):
                 forward(kind, off, t).wait_send()
                 forwarded(kind, off, t).wait_recv()
 
 
-def finish_kernel(ids_ref, q_ref, meta_ref, cent_ref, out_ref, count_ref):
+def finish_kernel(q_ref, meta_ref, cent_ref, out_ref, count_ref, ids, cents, mass, id_sem, cent_sem):
     contributions = q_ref.shape[0]
-    share = cent_ref.shape[0]
-    first = ids_ref[contributions] * share
-    out_ref[...] = PRIOR_WEIGHT * unit_rows(cent_ref[...])
-    count_ref[...] = jnp.zeros_like(count_ref)
+    share = cents.shape[0]
+    first = lax.axis_index("slab") * share
+    pull = pltpu.make_async_copy(meta_ref.at[:, 4], ids, id_sem)
+    pull.start()
+    load = pltpu.make_async_copy(cent_ref.at[pl.ds(first, share)], cents, cent_sem)
+    load.start()
+    mass[...] = jnp.zeros_like(mass)
+    load.wait()
+    out_ref[...] = PRIOR_WEIGHT * unit_rows(cents[...])
+    pull.wait()
     for start in range(0, contributions, 128):
         many = min(128, contributions - start)
         rows = jnp.concatenate([meta_ref[start : start + many, half, :] for half in range(CENT_BLK // 128)], axis=1)
@@ -242,15 +269,17 @@
             rows = jnp.concatenate([rows, jnp.zeros((128 - many, CENT_BLK), jnp.float32)], axis=0)
         scales = rows.T
         for k in range(many):
-            inner = ids_ref[start + k] - first
+            inner = ids[start + k, 0].astype(jnp.int32) - first
 
             @pl.when((inner >= 0) & (inner < share))
             def _():
                 out_ref[inner] += q_ref[start + k].astype(jnp.float32) * scales[:, k : k + 1]
                 parts = [meta_ref[start + k, 2 + half : 3 + half, :] for half in range(CENT_BLK // 128)]
-                count_ref[pl.ds(inner, 1), :] += jnp.concatenate(parts, axis=1)
-
-    masses = jnp.concatenate([count_ref[...], jnp.zeros((128 - share, CENT_BLK), jnp.float32)], axis=0).T
+                mass[pl.ds(inner, 1), :] += jnp.concatenate(parts, axis=1)
+
+    for half in range(CENT_BLK // 128):
+        count_ref[:, half, :] = mass[:, half * 128 : (half + 1) * 128]
+    masses = jnp.concatenate([mass[...], jnp.zeros((128 - share, CENT_BLK), jnp.float32)], axis=0).T
     for i in range(share):
         out_ref[i] = out_ref[i] / (masses[:, i : i + 1] + PRIOR_WEIGHT)
 
@@ -268,23 +297,24 @@
     fetched, req = pl.pallas_call(
         functools.partial(fetch_kernel, owners),
         out_shape=(jax.ShapeDtypeStruct((owners, CENT_BLK, width), jnp.bfloat16),
-                   jax.ShapeDtypeStruct((8, 128), jnp.int32)),
-        in_specs=[vmem, vmem],
+                   jax.ShapeDtypeStruct((1, 128), jnp.int32)),
+        in_specs=[vmem, anywhere],
         out_specs=(anywhere, vmem),
         scratch_shapes=[
-            pltpu.VMEM((owners, 8, 128), jnp.int32),
+            pltpu.VMEM(cents.shape, cents.dtype),
+            pltpu.VMEM((owners, 1, 128), jnp.int32),
             pltpu.SMEM((owners, 128), jnp.int32),
             pltpu.VMEM((owners, CENT_BLK, width), jnp.bfloat16),
-            dma((owners,)), dma((owners,)), dma, dma((owners,)), dma((owners,)), dma,
+            dma, dma((owners,)), dma((owners,)), dma, dma((owners,)), dma((owners,)), dma,
         ],
         compiler_params=pltpu.CompilerParams(
-            collective_id=0, has_side_effects=True, vmem_limit_bytes=16 * 2**20),
+            collective_id=0, has_side_effects=True, vmem_limit_bytes=60 * 2**20),
         name="fetch",
-    )(listed, cents)
+    )(listed.T, cents)
 
     group = 4
     packed, meta = pl.pallas_call(
-        functools.partial(softmax_kernel, group),
+        functools.partial(softmax_kernel, group, per_owner),
         out_shape=(jax.ShapeDtypeStruct((owners, CENT_BLK, width), jnp.int16),
                    jax.ShapeDtypeStruct((owners, 8, 128), jnp.float32)),
         grid_spec=pltpu.PrefetchScalarGridSpec(
@@ -307,9 +337,9 @@
             ],
         ),
         compiler_params=pltpu.CompilerParams(
-            dimension_semantics=("arbitrary",), vmem_limit_bytes=40 * 2**20),
+            dimension_semantics=("arbitrary",), vmem_limit_bytes=60 * 2**20),
         name="softmax",
-    )((listed // per_owner).reshape(-1), req[0], tokens.reshape(blocks, TOK_BLK, width), fetched)
+    )(listed.T, req, tokens.reshape(blocks, TOK_BLK, width), fetched)
 
     q_all, meta_all = pl.pallas_call(
         functools.partial(return_kernel, owners, slabs),
@@ -318,34 +348,28 @@
         in_specs=[anywhere, anywhere],
         out_specs=(anywhere, anywhere),
         scratch_shapes=[dma((2, owners)), dma((2, owners)), dma((2, slabs, owners)), dma((2, slabs, owners)), dma((2,))],
-        compiler_params=pltpu.CompilerParams(collective_id=1, has_side_effects=True),
+        compiler_params=pltpu.CompilerParams(
+            collective_id=1, has_side_effects=True, vmem_limit_bytes=60 * 2**20),
         name="give_back",
     )(packed, meta)
 
     contributions = slabs * owners
     meta_flat = meta_all.reshape(contributions, 8, 128)
-    ids = jnp.concatenate([meta_flat[:, 4, 0].astype(jnp.int32), lax.axis_index("slab").astype(jnp.int32)[None]])
     refined, counts = pl.pallas_call(
         finish_kernel,
         out_shape=(jax.ShapeDtypeStruct((share, CENT_BLK, width), jnp.float32),
-                   jax.ShapeDtypeStruct((share, CENT_BLK), jnp.float32)),
-        grid_spec=pltpu.PrefetchScalarGridSpec(
-            num_scalar_prefetch=1,
-            grid=(1,),
-            in_specs=[
-                pl.BlockSpec((contributions, CENT_BLK, width), lambda i, *_: (0, 0, 0)),
-                pl.BlockSpec((contributions, 8, 128), lambda i, *_: (0, 0, 0)),
-                pl.BlockSpec((share, CENT_BLK, width), lambda i, ids: (ids[contributions], 0, 0)),
-            ],
-            out_specs=[
-                pl.BlockSpec((share, CENT_BLK, width), lambda i, *_: (0, 0, 0)),
-                pl.BlockSpec((share, CENT_BLK), lambda i, *_: (0, 0)),
-            ],
-        ),
-        compiler_params=pltpu.CompilerParams(
-            dimension_semantics=("arbitrary",), vmem_limit_bytes=56 * 2**20),
+                   jax.ShapeDtypeStruct((share, CENT_BLK // 128, 128), jnp.float32)),
+        in_specs=[vmem, vmem, anywhere],
+        out_specs=(vmem, vmem),
+        scratch_shapes=[
+            pltpu.SMEM((contributions, 128), jnp.float32),
+            pltpu.VMEM((share, CENT_BLK, width), cents.dtype),
+            pltpu.VMEM((share, CENT_BLK), jnp.float32),
+            dma, dma,
+        ],
+        compiler_params=pltpu.CompilerParams(vmem_limit_bytes=60 * 2**20),
         name="finish",
-    )(ids, q_all.reshape(contributions, CENT_BLK, width), meta_flat, cents)
+    )(q_all.reshape(contributions, CENT_BLK, width), meta_flat, cents)
     return refined.reshape(share * CENT_BLK, width), counts.reshape(share * CENT_BLK)
 
 

time: 125 us -> 112 us (0.90)
  local copies, waits for them, and re-layouts: 7.7 us -> 0 us
  Pallas kernels: 114 us -> 111 us
  other arithmetic: 2.88 us -> 0 us
    unnamed x10 -> x0, local copies, waits for them, and re-layouts: 7.47 us -> none
    pallas_call x1, Pallas kernels: 41.3 us -> 34.8 us  [shards(): pl.pallas_call(functools.partial(return_kernel, owners, slabs), out_shape...]
    pallas_call x1, Pallas kernels: 28.9 us -> 31.5 us  [shards(): pl.pallas_call(functools.partial(softmax_kernel, group, per_owner), out_s...]
    convert_element_type x1 -> x0, other arithmetic: 1.56 us -> none  [shards(): meta_flat[:, 4, 0].astype(jnp.int32)]
where the time goes in v3:
time: 112 us; the launch traced here: 111 us
  Pallas kernels  111 us (99%)
    pallas_call x1, Pallas kernels, shards(): pl.pallas_call(functools.partial(fetch_kernel, owners), out_shape=(jax.Sh...  36.6 us
    pallas_call x1, Pallas kernels, shards(): pl.pallas_call(functools.partial(return_kernel, owners, slabs), out_shape...  34.8 us
    pallas_call x1, Pallas kernels, shards(): pl.pallas_call(functools.partial(softmax_kernel, group, per_owner), out_s...  31.5 us
    pallas_call x1, Pallas kernels, shards(): pl.pallas_call(finish_kernel, out_shape=(jax.ShapeDtypeStruct((share, CEN...  7.92 us

profile of v3, /device:TPU:0, one launch (start us, length us, event | category | flops | bytes accessed | tf_op | source)
XLA Modules:
  0.0 111.5 jit_solution(16313043977090040247)
XLA Ops:
  0.6 36.6 %fetch.1 = (bf16[16,256,128]{2,1,0:T(8,128)(2,1)}, s32[1,128]{1,0:T(1,128)}) custom-call(s32[3,64]{1,0:T(4,128)} %bitcast.12, bf16[32,256,128]{2,1,0:T(8,128)(2,1)} %bitcast.7), custom_call_target="tpu_custom_call" | custom-call | tf_op jit(solution)/shard_map/fetch/pallas_call | solution.py:297
  37.3 31.5 %softmax.1 = (s16[16,256,128]{2,1,0:T(8,128)(2,1)}, f32[16,8,128]{2,1,0:T(8,128)}) custom-call(s32[3,64]{1,0:T(4,128)} %bitcast.13, s32[1,128]{1,0:T(1,128)} %get-tuple-element.10.req_ref, bf16[64,256,128]{2,1,0:T(8,128)(2,1)} %bitcast.9, bf16[16,256,128]{2,1,0:T(8,128)(2,1)} %get-tuple-element.11.cent_ref), custom_call_target="tpu_custom_call" | custom-call | tf_op jit(solution)/shard_map/softmax/pallas_call | solution.py:316
  68.7 34.8 %give_back.1 = (s16[2,16,256,128]{3,2,1,0:T(8,128)(2,1)}, f32[2,16,8,128]{3,2,1,0:T(8,128)}) custom-call(s16[16,256,128]{2,1,0:T(8,128)(2,1)} %get-tuple-element.12.q_ref, f32[16,8,128]{2,1,0:T(8,128)} %get-tuple-element.13.meta_ref), custom_call_target="tpu_custom_call" | custom-call | tf_op jit(solution)/shard_map/give_back/pallas_call | solution.py:344
  103.5 7.9 %finish.1 = (f32[16,256,128]{2,1,0:T(8,128)}, f32[16,2,128]{2,1,0:T(2,128)}) custom-call(s16[32,256,128]{2,1,0:T(8,128)(2,1)} %bitcast.10, f32[32,8,128]{2,1,0:T(8,128)} %bitcast.11, bf16[32,256,128]{2,1,0:T(8,128)(2,1)} %bitcast.8), custom_call_target="tpu_custom_call" | custom-call | tf_op jit(solution)/shard_map/finish/pallas_call | solution.py:358

commit v4 on v3

--- a/solution.py
+++ b/solution.py
@@ -1,5 +1,4 @@
 import functools
-import math
 
 import jax
 import jax.numpy as jnp
@@ -102,11 +101,13 @@
         given_by(off).wait_recv()
 
 
-def softmax_kernel(group, per_owner, listed_ref, req_ref, tok_ref, cent_ref, q_ref, meta_ref, total, mass, grown, tok_held, scales):
+def softmax_kernel(group, unroll, per_owner, listed_ref, req_ref, tok_ref, cent_ref, q_ref, meta_ref, total, mass, grown, tok_held, scales):
     step = pl.program_id(0)
     owners = cent_ref.shape[0]
     width = tok_ref.shape[-1]
-    factor = math.log2(math.e) / (width * SOFTMAX_TEMP)
+    factor = 1.0 / (width * SOFTMAX_TEMP)
+    assert per_owner & (per_owner - 1) == 0
+    shift = per_owner.bit_length() - 1
 
     @pl.when(step == 0)
     def _():
@@ -116,34 +117,36 @@
         tok_held[1] = jnp.zeros_like(tok_held[1])
         scales[1] = jnp.zeros_like(scales[1])
 
+    def slot_of(j, block):
+        return listed_ref[j, block] >> shift
+
     def collect(block, side):
-        tok = tok_held[side]
-        scale = scales[side, 0:1]
+        weights = grown[side] * scales[side, 0:1]
+        part = weights[:, :128]
+        for lane in range(128, TOK_BLK, 128):
+            part = part + weights[:, lane : lane + 128]
+        sums = jnp.dot(weights.astype(jnp.bfloat16), tok_held[side], preferred_element_type=jnp.float32)
         for j in range(3):
-            slot = lax.div(listed_ref[j, block], per_owner)
-            weights = grown[side, j] * scale
-            part = weights[:, :128]
-            for lane in range(128, TOK_BLK, 128):
-                part = part + weights[:, lane : lane + 128]
-            mass[slot] += part
-            total[slot] += jnp.dot(weights.astype(jnp.bfloat16), tok, preferred_element_type=jnp.float32)
+            slot = slot_of(j, block)
+            mass[slot] += part[j * CENT_BLK : (j + 1) * CENT_BLK]
+            total[slot] += sums[j * CENT_BLK : (j + 1) * CENT_BLK]
 
     def grow(block, g, side):
         tok = unit_rows(tok_ref[g]).astype(jnp.bfloat16)
         tok_held[side] = tok
-        norm = jnp.zeros((1, TOK_BLK), jnp.float32)
-        for j in range(3):
-            scores = lax.dot_general(cent_ref[lax.div(listed_ref[j, block], per_owner)], tok, (((1,), (1,)), ((), ())),
-                                     preferred_element_type=jnp.float32)
-            value = jnp.exp2(scores * factor)
-            grown[side, j] = value
-            norm = norm + jnp.sum(value, axis=0, keepdims=True)
-        scales[side] = jnp.broadcast_to(1.0 / norm, (8, TOK_BLK))
-
-    for g in range(group):
-        block = step * group + g
-        collect(jnp.maximum(block - 1, 0), (g + 1) % 2)
-        grow(block, g, g % 2)
+        cents = jnp.concatenate([cent_ref[slot_of(j, block)] for j in range(3)], axis=0)
+        scores = lax.dot_general(cents, tok, (((1,), (1,)), ((), ())), preferred_element_type=jnp.float32)
+        value = jnp.exp(scores * factor)
+        grown[side] = value
+        scales[side] = jnp.broadcast_to(1.0 / jnp.sum(value, axis=0, keepdims=True), (8, TOK_BLK))
+
+    @pl.loop(0, group // unroll)
+    def _(turn):
+        for u in range(unroll):
+            g = turn * unroll + u
+            block = step * group + g
+            collect(jnp.maximum(block - 1, 0), (u + 1) % 2)
+            grow(block, g, u % 2)
 
     @pl.when(step == pl.num_programs(0) - 1)
     def _():
@@ -221,22 +224,26 @@
             for t in range(1, slabs):
                 forward(kind, off, t).start()
 
+    window = 3
     pass_on(0)
-    send(far[0])
-    for off in near:
-        send(off)
-    send(far[1])
+    for i in range(max(len(near), window)):
+        if i < len(near):
+            send(near[i])
+        if i < min(window, len(far)):
+            send(far[i])
+        if i == 1:
+            pass_on(near[0])
     for kind in range(2):
         own[kind].start()
-    ready = list(near)
+    ready = near[1:]
     for i, off in enumerate(far):
         pass_on_now, ready = ready[:2], ready[2:]
         for other in pass_on_now:
             pass_on(other)
         for kind in range(2):
             give(kind, off).wait_send()
-        if i + 2 < len(far):
-            send(far[i + 2])
+        if i + window < len(far):
+            send(far[i + window])
         ready.append(off)
     for off in ready:
         pass_on(off)
@@ -260,7 +267,8 @@
     load.start()
     mass[...] = jnp.zeros_like(mass)
     load.wait()
-    out_ref[...] = PRIOR_WEIGHT * unit_rows(cents[...])
+    for i in range(share):
+        out_ref[i] = PRIOR_WEIGHT * unit_rows(cents[i])
     pull.wait()
     for start in range(0, contributions, 128):
         many = min(128, contributions - start)
@@ -280,8 +288,9 @@
     for half in range(CENT_BLK // 128):
         count_ref[:, half, :] = mass[:, half * 128 : (half + 1) * 128]
     masses = jnp.concatenate([mass[...], jnp.zeros((128 - share, CENT_BLK), jnp.float32)], axis=0).T
+    inverse = 1.0 / (masses + PRIOR_WEIGHT)
     for i in range(share):
-        out_ref[i] = out_ref[i] / (masses[:, i : i + 1] + PRIOR_WEIGHT)
+        out_ref[i] = out_ref[i] * inverse[:, i : i + 1]
 
 
 def shards(owners, slabs, tokens, listed, centroids):
@@ -312,9 +321,10 @@
         name="fetch",
     )(listed.T, cents)
 
-    group = 4
+    group = min(16, blocks)
+    unroll = 4
     packed, meta = pl.pallas_call(
-        functools.partial(softmax_kernel, group, per_owner),
+        functools.partial(softmax_kernel, group, unroll, per_owner),
         out_shape=(jax.ShapeDtypeStruct((owners, CENT_BLK, width), jnp.int16),
                    jax.ShapeDtypeStruct((owners, 8, 128), jnp.float32)),
         grid_spec=pltpu.PrefetchScalarGridSpec(
@@ -331,7 +341,7 @@
             scratch_shapes=[
                 pltpu.VMEM((owners, CENT_BLK, width), jnp.float32),
                 pltpu.VMEM((owners, CENT_BLK, 128), jnp.float32),
-                pltpu.VMEM((2, 3, CENT_BLK, TOK_BLK), jnp.float32),
+                pltpu.VMEM((2, 3 * CENT_BLK, TOK_BLK), jnp.float32),
                 pltpu.VMEM((2, TOK_BLK, width), jnp.bfloat16),
                 pltpu.VMEM((2, 8, TOK_BLK), jnp.float32),
             ],

time: 112 us -> 105 us (0.938)
  Pallas kernels: 111 us -> 104 us
    pallas_call x1, Pallas kernels: 31.5 us -> 25.2 us  [shards(): pl.pallas_call(functools.partial(softmax_kernel, group, unroll, per_owner...]
where the time goes in v4:
time: 105 us
  Pallas kernels  104 us (99%)
    pallas_call x1, Pallas kernels, shards(): pl.pallas_call(functools.partial(fetch_kernel, owners), out_shape=(jax.Sh...  36.6 us
    pallas_call x1, Pallas kernels, shards(): pl.pallas_call(functools.partial(return_kernel, owners, slabs), out_shape...  35.1 us
    pallas_call x1, Pallas kernels, shards(): pl.pallas_call(functools.partial(softmax_kernel, group, unroll, per_owner...  25.2 us
    pallas_call x1, Pallas kernels, shards(): pl.pallas_call(finish_kernel, out_shape=(jax.ShapeDtypeStruct((share, CEN...  7.37 us

profile of v4, /device:TPU:0, one launch (start us, length us, event | category | flops | bytes accessed | tf_op | source)
XLA Modules:
  0.0 105.0 jit_solution(13785639094849211901)
XLA Ops:
  0.6 36.6 %fetch.1 = (bf16[16,256,128]{2,1,0:T(8,128)(2,1)}, s32[1,128]{1,0:T(1,128)}) custom-call(s32[3,64]{1,0:T(4,128)} %bitcast.12, bf16[32,256,128]{2,1,0:T(8,128)(2,1)} %bitcast.7), custom_call_target="tpu_custom_call" | custom-call | tf_op jit(solution)/shard_map/fetch/pallas_call | solution.py:306
  37.3 25.2 %softmax.1 = (s16[16,256,128]{2,1,0:T(8,128)(2,1)}, f32[16,8,128]{2,1,0:T(8,128)}) custom-call(s32[3,64]{1,0:T(4,128)} %bitcast.13, s32[1,128]{1,0:T(1,128)} %get-tuple-element.10.req_ref, bf16[64,256,128]{2,1,0:T(8,128)(2,1)} %bitcast.9, bf16[16,256,128]{2,1,0:T(8,128)(2,1)} %get-tuple-element.11.cent_ref), custom_call_target="tpu_custom_call" | custom-call | tf_op jit(solution)/shard_map/softmax/pallas_call | solution.py:326
  62.5 35.1 %give_back.1 = (s16[2,16,256,128]{3,2,1,0:T(8,128)(2,1)}, f32[2,16,8,128]{3,2,1,0:T(8,128)}) custom-call(s16[16,256,128]{2,1,0:T(8,128)(2,1)} %get-tuple-element.12.q_ref, f32[16,8,128]{2,1,0:T(8,128)} %get-tuple-element.13.meta_ref), custom_call_target="tpu_custom_call" | custom-call | tf_op jit(solution)/shard_map/give_back/pallas_call | solution.py:354
  97.6 7.4 %finish.1 = (f32[16,256,128]{2,1,0:T(8,128)}, f32[16,2,128]{2,1,0:T(2,128)}) custom-call(s16[32,256,128]{2,1,0:T(8,128)(2,1)} %bitcast.10, f32[32,8,128]{2,1,0:T(8,128)} %bitcast.11, bf16[32,256,128]{2,1,0:T(8,128)(2,1)} %bitcast.8), custom_call_target="tpu_custom_call" | custom-call | tf_op jit(solution)/shard_map/finish/pallas_call | solution.py:368

commit v5 on v4

--- a/solution.py
+++ b/solution.py
@@ -257,7 +257,8 @@
                 forwarded(kind, off, t).wait_recv()
 
 
-def finish_kernel(q_ref, meta_ref, cent_ref, out_ref, count_ref, ids, cents, mass, id_sem, cent_sem):
+def finish_kernel(q_hbm, meta_ref, cent_ref, out_hbm, count_ref, ids, cents, mass, q_ref, out_ref,
+                  id_sem, cent_sem, q_sem, out_sem):
     contributions = q_ref.shape[0]
     share = cents.shape[0]
     first = lax.axis_index("slab") * share
@@ -265,11 +266,14 @@
     pull.start()
     load = pltpu.make_async_copy(cent_ref.at[pl.ds(first, share)], cents, cent_sem)
     load.start()
+    bring = pltpu.make_async_copy(q_hbm, q_ref, q_sem)
+    bring.start()
     mass[...] = jnp.zeros_like(mass)
     load.wait()
     for i in range(share):
         out_ref[i] = PRIOR_WEIGHT * unit_rows(cents[i])
     pull.wait()
+    bring.wait()
     for start in range(0, contributions, 128):
         many = min(128, contributions - start)
         rows = jnp.concatenate([meta_ref[start : start + many, half, :] for half in range(CENT_BLK // 128)], axis=1)
@@ -289,8 +293,12 @@
         count_ref[:, half, :] = mass[:, half * 128 : (half + 1) * 128]
     masses = jnp.concatenate([mass[...], jnp.zeros((128 - share, CENT_BLK), jnp.float32)], axis=0).T
     inverse = 1.0 / (masses + PRIOR_WEIGHT)
+    leave = [pltpu.make_async_copy(out_ref.at[i], out_hbm.at[i], out_sem.at[i]) for i in range(share)]
     for i in range(share):
         out_ref[i] = out_ref[i] * inverse[:, i : i + 1]
+        leave[i].start()
+    for i in range(share):
+        leave[i].wait()
 
 
 def shards(owners, slabs, tokens, listed, centroids):
@@ -322,7 +330,7 @@
     )(listed.T, cents)
 
     group = min(16, blocks)
-    unroll = 4
+    unroll = 8
     packed, meta = pl.pallas_call(
         functools.partial(softmax_kernel, group, unroll, per_owner),
         out_shape=(jax.ShapeDtypeStruct((owners, CENT_BLK, width), jnp.int16),
@@ -369,13 +377,15 @@
         finish_kernel,
         out_shape=(jax.ShapeDtypeStruct((share, CENT_BLK, width), jnp.float32),
                    jax.ShapeDtypeStruct((share, CENT_BLK // 128, 128), jnp.float32)),
-        in_specs=[vmem, vmem, anywhere],
-        out_specs=(vmem, vmem),
+        in_specs=[anywhere, vmem, anywhere],
+        out_specs=(anywhere, vmem),
         scratch_shapes=[
             pltpu.SMEM((contributions, 128), jnp.float32),
             pltpu.VMEM((share, CENT_BLK, width), cents.dtype),
             pltpu.VMEM((share, CENT_BLK), jnp.float32),
-            dma, dma,
+            pltpu.VMEM((contributions, CENT_BLK, width), jnp.int16),
+            pltpu.VMEM((share, CENT_BLK, width), jnp.float32),
+            dma, dma, dma, dma((share,)),
         ],
         compiler_params=pltpu.CompilerParams(vmem_limit_bytes=60 * 2**20),
         name="finish",

time: 105 us -> 102 us (0.971)
  Pallas kernels: 104 us -> 101 us
    pallas_call x1, Pallas kernels: 25.2 us -> 21.8 us  [shards(): pl.pallas_call(functools.partial(softmax_kernel, group, unroll, per_owner...]
where the time goes in v5:
time: 102 us
  Pallas kernels  101 us (99%)
    pallas_call x1, Pallas kernels, shards(): pl.pallas_call(functools.partial(fetch_kernel, owners), out_shape=(jax.Sh...  36.6 us
    pallas_call x1, Pallas kernels, shards(): pl.pallas_call(functools.partial(return_kernel, owners, slabs), out_shape...  35.1 us
    pallas_call x1, Pallas kernels, shards(): pl.pallas_call(functools.partial(softmax_kernel, group, unroll, per_owner...  21.8 us
    pallas_call x1, Pallas kernels, shards(): pl.pallas_call(finish_kernel, out_shape=(jax.ShapeDtypeStruct((share, CEN...  7.78 us

profile of v5, /device:TPU:0, one launch (start us, length us, event | category | flops | bytes accessed | tf_op | source)
XLA Modules:
  0.0 102.0 jit_solution(11639126352042437060)
XLA Ops:
  0.6 36.6 %fetch.1 = (bf16[16,256,128]{2,1,0:T(8,128)(2,1)}, s32[1,128]{1,0:T(1,128)}) custom-call(s32[3,64]{1,0:T(4,128)} %bitcast.12, bf16[32,256,128]{2,1,0:T(8,128)(2,1)} %bitcast.7), custom_call_target="tpu_custom_call" | custom-call | tf_op jit(solution)/shard_map/fetch/pallas_call | solution.py:314
  37.3 21.8 %softmax.1 = (s16[16,256,128]{2,1,0:T(8,128)(2,1)}, f32[16,8,128]{2,1,0:T(8,128)}) custom-call(s32[3,64]{1,0:T(4,128)} %bitcast.13, s32[1,128]{1,0:T(1,128)} %get-tuple-element.10.req_ref, bf16[64,256,128]{2,1,0:T(8,128)(2,1)} %bitcast.9, bf16[16,256,128]{2,1,0:T(8,128)(2,1)} %get-tuple-element.11.cent_ref), custom_call_target="tpu_custom_call" | custom-call | tf_op jit(solution)/shard_map/softmax/pallas_call | solution.py:334
  59.1 35.1 %give_back.1 = (s16[2,16,256,128]{3,2,1,0:T(8,128)(2,1)}, f32[2,16,8,128]{3,2,1,0:T(8,128)}) custom-call(s16[16,256,128]{2,1,0:T(8,128)(2,1)} %get-tuple-element.12.q_ref, f32[16,8,128]{2,1,0:T(8,128)} %get-tuple-element.13.meta_ref), custom_call_target="tpu_custom_call" | custom-call | tf_op jit(solution)/shard_map/give_back/pallas_call | solution.py:362
  94.2 7.8 %finish.1 = (f32[16,256,128]{2,1,0:T(8,128)}, f32[16,2,128]{2,1,0:T(2,128)}) custom-call(s16[32,256,128]{2,1,0:T(8,128)(2,1)} %bitcast.10, f32[32,8,128]{2,1,0:T(8,128)} %bitcast.11, bf16[32,256,128]{2,1,0:T(8,128)(2,1)} %bitcast.8), custom_call_target="tpu_custom_call" | custom-call | tf_op jit(solution)/shard_map/finish/pallas_call | solution.py:376
